TPU v7x, 32 devices: a whole 2x2x4 slice. The times are simulated.
32 devices in a mesh: groups: 2 (over y), chan: 4 (over z), tok: 4 (over x, core).
Axes of the slice: x: 2, y: 2, z: 4, core: 2. Of those that a mesh axis runs over, the one named last changes fastest.
Arguments:
- hidden: bfloat16 [2560, 8192], P(('groups', 'tok'), 'chan'), parts along dimension 0, may hold values from -6 to 6
- norm_gain: bfloat16 [8192], replicated, may hold values from 0.099609375 to 1.8984375
- w_in: bfloat16 [8192, 3, 8192], P('tok', None, 'chan'), may hold values from -0.0625 to 0.0625
- short_taps: float32 [3, 7, 8192], P(None, None, 'chan'), may hold values from -3 to 3
- mr_filter: float32 [512, 128], P('chan'), may hold values from -0.5 to 0.5
- skip_gain: float32 [8192], P('chan'), may hold values from 0.5 to 1.5
- u_store: bfloat16 [64, 127, 8192], P(('groups', 'tok'), None, 'chan'), parts along dimension 0, may hold values from -6 to 6
- z_store: bfloat16 [64, 6, 3, 8192], P(('groups', 'tok'), None, None, 'chan'), parts along dimension 0, may hold values from -6 to 6
- holder: int32 [16], P('groups'), parts along dimension 0, may hold values from 0 to 3
- slot: int32 [16], P('groups'), parts along dimension 0, may hold values from 0 to 7
Outputs:
- gated_out: bfloat16 [2560, 8192], P(('groups', 'tok'), 'chan'), parts along dimension 0
There are 2 independent parts, one for each index of `groups`. A program takes and returns all parts, laid end to end along the dimension named above; an argument that names none is the same for every part. Nothing has to cross between parts.
Inputs may be any that keep to these rules, and one draw needn't show every extreme that they name: `holder`: index of a token shard. Index of a slot on the holder.
All inputs are finite; a program needn't handle non-finite values.
Results may differ from a plain program's by a relative error of at most 0.0086.
Values may be sent and summed in bfloat16 or wider, within the bound.
A program may use at most 448 MiB of HBM per device.

v0:
```python
import jax
import jax.numpy as jnp
from jax import lax
from jax.sharding import PartitionSpec as P

GROUP = 16
FILTER = 128
SHORT = 7


def short_filter(z_ext, taps):
    count = z_ext.shape[1] - (SHORT - 1)
    total = jnp.zeros((z_ext.shape[0], count, z_ext.shape[2], z_ext.shape[3]), jnp.float32)
    for lag in range(SHORT):
        begin = SHORT - 1 - lag
        total = total + taps[:, lag, :] * z_ext[:, begin : begin + count]
    return total


def long_filter(u_ext, filters):
    prompts, length, chans = u_ext.shape
    count = length - (FILTER - 1)
    rows_t = jnp.arange(count, dtype=jnp.int32)[:, None]
    cols_s = jnp.arange(length, dtype=jnp.int32)[None, :]
    lagged = rows_t + (FILTER - 1) - cols_s
    valid = (lagged >= 0) & (lagged < FILTER)
    table = jnp.take(filters, jnp.clip(lagged, 0, FILTER - 1), axis=1)
    table = jnp.where(valid[None], table, jnp.float32(0.0))
    grouped = u_ext.reshape(prompts, length, chans // GROUP, GROUP)
    result = jnp.einsum("gts,psgc->ptgc", table, grouped, precision=lax.Precision.HIGHEST)
    return result.reshape(prompts, count, chans)


def on_device(
    hidden, norm_gain, w_in, short_taps, mr_filter, skip_gain, u_store, z_store, holder, slot
):
    rows = hidden.shape[0]
    chans = hidden.shape[1]
    tok_count = lax.axis_size("tok")
    per_shard = holder.shape[0] // tok_count
    new_len = rows // per_shard
    whole = lax.all_gather(hidden, "chan", axis=1, tiled=True)
    values = whole.astype(jnp.float32)
    meansq = jnp.mean(values * values, axis=-1, keepdims=True)
    normed = (values * lax.rsqrt(meansq + 1e-06) * norm_gain.astype(jnp.float32)).astype(
        jnp.bfloat16
    )
    piece = lax.all_gather(w_in, "tok", axis=0, tiled=True)
    height = piece.shape[0]
    projected = jnp.dot(
        normed, piece.reshape(height, 3 * chans), preferred_element_type=jnp.float32
    )
    streams = projected.astype(jnp.bfloat16).reshape(per_shard, new_len, 3, chans)
    first = lax.axis_index("tok") * per_shard
    mine_holder = lax.dynamic_slice_in_dim(holder, first, per_shard)
    mine_slot = lax.dynamic_slice_in_dim(slot, first, per_shard)
    slot_count = u_store.shape[0]
    entry = mine_holder * slot_count + mine_slot
    start_u = jnp.zeros((per_shard,) + u_store.shape[1:], jnp.bfloat16)
    start_z = jnp.zeros((per_shard,) + z_store.shape[1:], jnp.bfloat16)
    pieces = (
        lax.all_gather(u_store, "tok", axis=0, tiled=True),
        lax.all_gather(z_store, "tok", axis=0, tiled=True),
    )
    count = pieces[0].shape[0]
    inside = (entry >= 0) & (entry < count)
    index = jnp.clip(entry, 0, count - 1)
    new_u = jnp.where(inside[:, None, None], pieces[0][index], start_u)
    new_z = jnp.where(inside[:, None, None, None], pieces[1][index], start_z)
    z_ext = jnp.concatenate([new_z, streams], axis=1).astype(jnp.float32)
    filtered = short_filter(z_ext, short_taps)
    gated = (filtered[:, :, 1] * filtered[:, :, 2]).astype(jnp.bfloat16)
    u_ext = jnp.concatenate([new_u, gated], axis=1).astype(jnp.float32)
    mixed = long_filter(u_ext, mr_filter) + skip_gain * gated.astype(jnp.float32)
    output = (filtered[:, :, 0] * mixed).astype(jnp.bfloat16)
    return output.reshape(rows, chans)


def solution(mesh):
    placed = (
        P(("groups", "tok"), "chan"),
        P(),
        P("tok", None, "chan"),
        P(None, None, "chan"),
        P("chan", None),
        P("chan"),
        P(("groups", "tok"), None, "chan"),
        P(("groups", "tok"), None, None, "chan"),
        P("groups"),
        P("groups"),
    )
    return jax.shard_map(
        on_device,
        mesh=mesh,
        in_specs=placed,
        out_specs=P(("groups", "tok"), "chan"),
        check_vma=False,
    )
```

profile of v0, /device:TPU:0, one launch (start us, length us, event | category | flops | bytes accessed | tf_op | source)
XLA Modules:
  0.0 988.7 jit_solution(4295289439357870650)
XLA Ops:
  6.5 0.0 all-gather.5.cloned.1.call-start
  6.5 0.7 all-gather.5.cloned.1.call-update
  7.3 0.0 all-gather.7.cloned.1.call-start
  7.3 0.7 all-gather.7.cloned.1.call-update
  8.0 0.0 all-gather.11.cloned.1.call-start
  8.1 0.7 all-gather.11.cloned.1.call-update
  8.7 0.0 all-gather.9.cloned.1.call-start
  8.8 33.3 %copy.43 = bf16[2048,3,2048]{0,2,1:T(8,128)(2,1)} copy(bf16[2048,3,2048]{2,0,1:T(8,128)(2,1)} %param.12) | data formatting | bytes 50331648 | tf_op args[2]
  42.1 0.0 copy-start.4
  42.1 0.0 copy-start
  42.1 0.0 copy-start.2
  42.1 0.0 all-gather.9.cloned.1.call-update
  42.1 0.7 copy-done.4
  42.8 0.6 convert_element_type.37
  43.4 0.0 copy-done
  43.4 0.1 fusion.31
  43.5 0.6 copy.77
  44.2 0.1 compare_select_fusion
  44.3 0.3 reshape.154
  44.7 0.0 copy-done.2
  44.7 0.1 copy.50
  44.8 152.5 %gather_fusion.2 = f32[45920,128]{1,0:T(8,128)} fusion(f32[128,128]{0,1:T(8,128)S(1)} %copy.50, s32[46080]{0:T(1024)S(1)} %pad_clamp_fusion), kind=kCustom, calls=%fused_computation.2 | custom fusion | bytes 47205760 | tf_op jit(solution)/shard_map/jit(_take)/gather | solution.py:27
  197.3 23.2 %reshape.157 = f32[160,287,128]{2,1,0:T(8,128)} reshape(f32[45920,128]{1,0:T(8,128)} %gather_fusion.2) | data formatting | bytes 47022080 | tf_op jit(solution)/shard_map/jit(_take)/gather | solution.py:27
  220.5 0.2 fusion.27
  220.8 18.4 %select_bitcast_fusion = f32[128,160,287,1]{0,2,1,3:T(8,128)} fusion(f32[160,287,128]{2,1,0:T(8,128)} %reshape.157, pred[160,287]{1,0:T(8,128)(4,1)S(1)} %get-tuple-element.17, pred[160,287]{1,0:T(8,128)(4,1)S(1)} %get-tuple-element.16), kind=kLoop, calls=%fused_computation.3 | loop fusion | flops 11755520 | bytes 47113920 | tf_op jit(solution)/shard_map/jit(_where)/select_n | solution.py:28
  239.1 0.0 copy-start.6
  239.1 0.0 copy-start.7
  239.1 30.7 %copy.54 = f32[128,160,287,1]{2,1,3,0:T(8,128)} copy(f32[128,160,287,1]{0,2,1,3:T(8,128)} %select_bitcast_fusion) | data formatting | bytes 47022080 | tf_op jit(solution)/shard_map/jit(_where)/select_n | solution.py:28
  269.9 0.0 copy-done.6
  269.9 0.0 copy-done.7
  269.9 0.1 compare_and_fusion
  270.1 0.0 all-gather.5.cloned.1.call-done
  270.1 3.8 copy.42
  273.9 0.6 gather_fusion
  274.5 0.1 broadcast_select_fusion
  274.6 0.1 copy.44
  274.7 0.0 all-gather.7.cloned.1.call-done
  274.8 4.6 fusion
  279.4 0.0 copy-start.3
  279.4 0.0 all-gather.11.cloned.1.call-done
  279.4 20.6 %copy.45 = bf16[32,127,2048]{2,1,0:T(8,128)(2,1)} copy(bf16[32,127,2048]{2,0,1:T(8,128)(2,1)} %all-gather.11.cloned.1.call-done) | data formatting | bytes 33292288 | tf_op jit(solution)/shard_map/all_gather | solution.py:62
  300.1 8.3 gather_fusion.1
  308.4 0.7 copy.46
  309.1 1.1 copy_select_fusion
  310.2 515.7 %all-gather.9.cloned.1.call-done = bf16[8192,3,2048]{0,2,1:T(8,128)(2,1)} async-done(((bf16[2048,3,2048]{0,2,1:T(8,128)(2,1)}), bf16[8192,3,2048]{0,2,1:T(8,128)(2,1)}) %all-gather.9.cloned.1.call-update) | async-done | bytes 100663312 | tf_op jit(solution)/shard_map/all_gather | solution.py:48
  825.9 0.0 copy-done.3
  825.9 43.0 %convolution_convert_fusion = bf16[320,6144]{1,0:T(8,128)(2,1)} fusion(bf16[8192,6144]{0,1:T(8,128)(2,1)} %bitcast, bf16[320,8192]{1,0:T(8,128)(2,1)} %all-gather.7.cloned.1.call-done, f32[8192]{0:T(1024)S(1)} %copy-done.3, f32[320]{0:T(512)S(1)} %add_rsqrt_fusion), kind=kOutput, calls=%fused_computation.22 | convolution fusion | flops 32224706560 | bytes 109872384 | tf_op jit(solution)/shard_map/dot_general | solution.py:50
  868.9 0.0 copy-start.1
  868.9 12.1 %reshape.133 = bf16[2,160,3,2048]{3,2,1,0:T(4,128)(2,1)} reshape(bf16[320,6144]{1,0:T(8,128)(2,1)} %convolution_convert_fusion) | data formatting | bytes 7864320 | tf_op jit(solution)/shard_map/reshape | solution.py:53
  881.0 9.8 maximum_convert_fusion
  890.7 0.0 copy-done.1
  890.7 30.4 %fusion.3 = f32[2,160,3,2048]{3,2,1,0:T(4,128)S(1)} fusion(f32[2,166,3,2048]{3,2,1,0:T(4,128)} %maximum_convert_fusion, f32[3,2048]{1,0:T(4,128)S(1)} %get-tuple-element.18, f32[3,2048]{1,0:T(4,128)S(1)} %get-tuple-element.19, f32[3,2048]{1,0:T(4,128)S(1)} %get-tuple-element.20, f32[3,2048]{1,0:T(4,128)S(1)} %get-tuple-element.21, ...), kind=kLoop, calls=%fused_computation.10 | loop fusion | flops 25559040 | bytes 63086592 | tf_op jit(solution)/shard_map/add | solution.py:16
  921.1 6.2 fusion.30
  927.3 4.0 copy.48
  931.3 2.8 copy.65
  934.1 25.1 %fusion.20 = f32[2,160,128,16]{1,3,0,2:T(8,128)} fusion(f32[128,160,287,1]{2,1,3,0:T(8,128)} %copy.54, bf16[2,127,128,16]{1,3,0,2:T(8,128)(2,1)} %copy_select_fusion, bf16[2,160,128,16]{1,3,2,0:T(8,128)(2,1)} %bitcast.41), kind=kOutput, calls=%fused_computation.36 | convolution fusion | flops 2261762048 | bytes 28483584 | tf_op jit(solution)/shard_map/gts,psgc->ptgc/dot_general | solution.py:30
  959.3 8.3 copy.52
  967.5 0.0 copy-start.5
  967.5 5.1 reshape.134
  972.6 2.3 copy.53
  974.9 2.9 copy.64
  977.8 0.0 copy-done.5
  977.8 4.3 fusion.19
  (8 shorter events, 0.1 us)
Async XLA Ops:
  6.5 263.6 %all-gather.5.cloned.1.call-start = ((), (), s32[]{:S(2)}) async-start(), calls=%async_computation | async-start | bytes 2949120 | tf_op jit(solution)/shard_map/all_gather | solution.py:63
  7.3 267.5 %all-gather.7.cloned.1.call-start = ((), (), s32[]{:S(2)}) async-start(), calls=%async_computation.1 | async-start | bytes 6553600 | tf_op jit(solution)/shard_map/all_gather | solution.py:42
  8.0 271.4 %all-gather.11.cloned.1.call-start = ((), (), s32[]{:S(2)}) async-start(), calls=%async_computation.3 | async-start | bytes 20807680 | tf_op jit(solution)/shard_map/all_gather | solution.py:62
  8.7 817.1 %all-gather.9.cloned.1.call-start = ((), (), s32[]{:S(2)}) async-start(), calls=%async_computation.2 | async-start | bytes 125829120 | tf_op jit(solution)/shard_map/all_gather | solution.py:48
  42.1 0.7 copy-start.4
  42.1 1.3 copy-start
  42.1 2.6 copy-start.2
  239.1 30.7 %copy-start.6 = (s32[8]{0:T(128)S(1)}, s32[8]{0:T(128)}, u32[]{:S(2)}) copy-start(s32[8]{0:T(128)} %param.19) | copy-start | bytes 100
  239.1 30.7 %copy-start.7 = (s32[8]{0:T(128)S(1)}, s32[8]{0:T(128)}, u32[]{:S(2)}) copy-start(s32[8]{0:T(128)} %param.18) | copy-start | bytes 100
  279.4 546.5 %copy-start.3 = (f32[8192]{0:T(1024)S(1)}, f32[8192]{0:T(1024)}, u32[]{:S(2)}) copy-start(f32[8192]{0:T(1024)} %convert_element_type.37) | copy-start | bytes 98308
  868.9 21.9 %copy-start.1 = (f32[3,1,2048]{2,0,1:T(4,128)S(1)}, f32[3,1,2048]{2,0,1:T(4,128)}, u32[]{:S(2)}) copy-start(f32[3,1,2048]{2,0,1:T(4,128)} %copy.77) | copy-start | bytes 73732
  967.5 10.3 %copy-start.5 = (f32[2048]{0:T(1024)S(1)}, f32[2048]{0:T(1024)}, u32[]{:S(2)}) copy-start(f32[2048]{0:T(1024)} %param.15) | copy-start | bytes 24580
Sparse Core Ops, SparseCore 0:
  8.9 26.7 all-gather.4
  37.3 98.0 all-gather.6
  137.0 103.4 all-gather.10
  241.9 583.9 all-gather.8
where the time goes:
time: 992 us; the launch traced here: 989 us
  waiting for transfers between devices  518 us (52%)
  local copies, waits for them, and re-layouts  313 us (32%)
  other arithmetic  75.9 us (8%)
  matrix products  68.1 us (7%)
  between operations  13.3 us (1%)
    all_gather x1, waiting for transfers between devices, on_device(): piece = lax.all_gather(w_in, 'tok', axis=0, tiled=True)  516 us
    gather x2, local copies, waits for them, and re-layouts, long_filter(): table = jnp.take(filters, jnp.clip(lagged, 0, FILTER - 1), axis=1)  176 us
    dot_general x1, matrix products, on_device(): jnp.dot(normed, piece.reshape(height, 3 * chans), preferred_element_type=...  43 us
    unnamed x24, local copies, waits for them, and re-layouts  40.5 us
    select_n x1, local copies, waits for them, and re-layouts, long_filter(): table = jnp.where(valid[None], table, jnp.float32(0.0))  30.7 us
    add x1, other arithmetic, short_filter(): total = total + taps[:, lag, :] * z_ext[:, begin:begin + count]  30.4 us
    dot_general x1, matrix products, long_filter(): jnp.einsum('gts,psgc->ptgc', table, grouped, precision=lax.Precision.HIGH...  25.1 us
    all_gather x1, local copies, waits for them, and re-layouts, on_device(): lax.all_gather(u_store, 'tok', axis=0, tiled=True)  20.6 us
  transfers between devices with their start and end apart: 4, of which 1 were waited for; matrix products, arithmetic and copies ran while one was open for 30% of the time, Pallas kernels for 0%

commit v1 on v0

v1 whole, which is shorter than its diff:
```python
import functools

import jax
import jax.numpy as jnp
from jax import lax
from jax.experimental import pallas as pl
from jax.experimental.pallas import tpu as pltpu
from jax.sharding import PartitionSpec as P

GROUP = 16
FILTER = 128
SHORT = 7
PAD = 16


def swap(value, count, mask):
    return lax.ppermute(value, "tok", [(i, i ^ mask) for i in range(count)])


def mix_kernel(count, new_len, *refs):
    parts, (z_ref, u_ref, taps_ref, filt_ref, skip_ref, out_ref, z_scr, u_scr) = refs[:count], refs[count:]
    tile = out_ref.shape[1]
    prompts = z_ref.shape[0]
    groups = tile // GROUP
    lane_group = lax.broadcasted_iota(jnp.int32, (FILTER, tile), 1) // GROUP
    rest = new_len - FILTER

    def short(p, s):
        rows = pl.ds(p * new_len, new_len)
        total = parts[0][s, rows, :].astype(jnp.float32)
        for part in parts[1:]:
            total = total + part[s, rows, :].astype(jnp.float32)
        z_scr[0:PAD, :] = z_ref[p, s * PAD : (s + 1) * PAD, :].astype(jnp.float32)
        z_scr[PAD : PAD + new_len, :] = total.astype(jnp.bfloat16).astype(jnp.float32)
        acc = taps_ref[s, 0:1, :] * z_scr[PAD : PAD + new_len, :]
        for lag in range(1, SHORT):
            acc = acc + taps_ref[s, lag : lag + 1, :] * z_scr[PAD - lag : PAD - lag + new_len, :]
        return acc

    for p in range(prompts):
        gated = (short(p, 1) * short(p, 2)).astype(jnp.bfloat16)
        u_scr[0:FILTER, :] = u_ref[p]
        u_scr[FILTER : FILTER + new_len, :] = gated
        early = jnp.zeros((FILTER, tile), jnp.float32)
        late = jnp.zeros((rest, tile), jnp.float32)
        first = u_scr[0 : 2 * FILTER, :]
        second = u_scr[FILTER : FILTER + new_len, :]
        for g in range(groups):
            line = jnp.broadcast_to(filt_ref[g : g + 1, :], (FILTER, 2 * FILTER))
            table = pltpu.roll(line, 0, 1, stride=1, stride_axis=0).astype(jnp.bfloat16)
            a = jnp.dot(table, first, preferred_element_type=jnp.float32)
            b = jnp.dot(table[0:rest, 0:new_len], second, preferred_element_type=jnp.float32)
            early = jnp.where(lane_group == g, a, early)
            late = jnp.where(lane_group[0:rest] == g, b, late)
        mixed = jnp.concatenate([early, late], axis=0) + skip_ref[...] * gated.astype(jnp.float32)
        out_ref[p * new_len : (p + 1) * new_len, :] = (short(p, 0) * mixed).astype(jnp.bfloat16)


def mix(parts, z_tail, u_tail, taps, filters, skip, base, width, new_len):
    rows = parts[0].shape[1]
    prompts = z_tail.shape[0]
    tile = min(256, width)
    off = base // tile
    body = functools.partial(mix_kernel, len(parts), new_len)
    return pl.pallas_call(
        body,
        grid=(width // tile,),
        out_shape=jax.ShapeDtypeStruct((rows, width), jnp.bfloat16),
        in_specs=[pl.BlockSpec((3, rows, tile), lambda i: (0, 0, i)) for _ in parts]
        + [
            pl.BlockSpec((prompts, 3 * PAD, tile), lambda i: (0, 0, i + off)),
            pl.BlockSpec((prompts, FILTER, tile), lambda i: (0, 0, i + off)),
            pl.BlockSpec((3, SHORT, tile), lambda i: (0, 0, i + off)),
            pl.BlockSpec((tile // GROUP, 2 * FILTER), lambda i: (i + off, 0)),
            pl.BlockSpec((1, tile), lambda i: (0, i + off)),
        ],
        out_specs=pl.BlockSpec((rows, tile), lambda i: (0, i)),
        scratch_shapes=[
            pltpu.VMEM((PAD + new_len, tile), jnp.float32),
            pltpu.VMEM((FILTER + new_len, tile), jnp.bfloat16),
        ],
        compiler_params=pltpu.CompilerParams(vmem_limit_bytes=32 * 1024 * 1024),
        cost_estimate=pl.CostEstimate(
            flops=2 * rows * width * 256 * 20, bytes_accessed=rows * width * 32, transcendentals=0
        ),
    )(*parts, z_tail, u_tail, taps, filters, skip)


def tails(u_store, z_store, holder, slot, count, per_shard):
    me = lax.axis_index("tok")
    chans = u_store.shape[2]
    slots = u_store.shape[0]
    z_rows = jnp.transpose(z_store, (0, 2, 1, 3))
    z_rows = jnp.pad(z_rows, ((0, 0), (0, 0), (PAD - (SHORT - 1), 0), (0, 0)))
    z_rows = z_rows.reshape(slots, 3 * PAD, chans)
    u_rows = jnp.pad(u_store, ((0, 0), (1, 0), (0, 0)))
    blocks, keys = [], []
    for s in range(count):
        begin = (me ^ s) * per_shard
        own_slot = lax.dynamic_slice_in_dim(slot, begin, per_shard)
        keys.append(lax.dynamic_slice_in_dim(holder, begin, per_shard))
        rows = [
            jnp.concatenate(
                [
                    lax.dynamic_index_in_dim(u_rows, own_slot[p], 0, keepdims=False),
                    lax.dynamic_index_in_dim(z_rows, own_slot[p], 0, keepdims=False),
                ],
                axis=0,
            )
            for p in range(per_shard)
        ]
        blocks.append(jnp.stack(rows))
    keys = jnp.stack(keys)
    held = jnp.stack(blocks)
    bit = 0
    while (1 << bit) < count:
        mask = 1 << bit
        got = swap(held[1::2], count, mask)
        keys = keys[0::2]
        take = (keys >> bit) == ((me ^ mask) >> bit)
        held = jnp.where(take[:, :, None, None], got, held[0::2])
        bit += 1
    held = held[0]
    return held[:, 0:FILTER], held[:, FILTER:]


def on_device(
    hidden, norm_gain, w_in, short_taps, mr_filter, skip_gain, u_store, z_store, holder, slot
):
    rows = hidden.shape[0]
    chans = hidden.shape[1]
    depth = w_in.shape[0]
    count = lax.axis_size("tok")
    me = lax.axis_index("tok")
    per_shard = holder.shape[0] // count
    new_len = rows // per_shard
    u_tail, z_tail = tails(u_store, z_store, holder, slot, count, per_shard)
    weights = jnp.transpose(w_in, (1, 0, 2))
    filters = jnp.pad(mr_filter[:, ::-1], ((0, 0), (1, FILTER - 1)))
    skip = skip_gain.reshape(1, chans)
    gain = norm_gain.astype(jnp.float32)
    chunks = max(1, min(4, chans // 512))
    width = chans // chunks
    order = [s for s in range(count) if s & 1] + [s for s in range(count) if not s & 1]
    half = count // 2
    wholes = [
        lax.all_gather(hidden[p * new_len : (p + 1) * new_len], "chan", axis=1, tiled=True)
        for p in range(per_shard)
    ]
    results = []
    for p in range(per_shard):
        values = wholes[p].astype(jnp.float32)
        meansq = jnp.mean(values * values, axis=-1, keepdims=True)
        normed = (values * lax.rsqrt(meansq + 1e-06) * gain).astype(jnp.bfloat16)
        got = {}
        for s in range(count):
            mine = lax.dynamic_slice_in_dim(normed, (me ^ s) * depth, depth, 1)
            got[s] = mine if s == 0 else swap(mine, count, s)
        leave = jnp.concatenate([got[s] for s in order[:half]], axis=0)
        keep = jnp.concatenate([got[s] for s in order[half:]], axis=0)
        pieces = []
        for c in range(chunks):
            part = weights[:, :, c * width : (c + 1) * width]
            sent = jnp.stack(
                [jnp.dot(leave, part[s], preferred_element_type=jnp.float32) for s in range(3)]
            ).astype(jnp.bfloat16)
            kept = jnp.stack(
                [jnp.dot(keep, part[s], preferred_element_type=jnp.float32) for s in range(3)]
            )
            held = kept.reshape(3, half, new_len, width)
            back = swap(sent, count, 1).reshape(3, half, new_len, width)
            bit = 1
            while (1 << bit) < count:
                now = held + back.astype(jnp.float32)
                out = now[:, 1::2].astype(jnp.bfloat16)
                held = now[:, 0::2]
                back = swap(out, count, 1 << bit)
                bit += 1
            pieces.append(
                mix(
                    [held[:, 0], back[:, 0]],
                    z_tail[p : p + 1],
                    u_tail[p : p + 1],
                    short_taps,
                    filters,
                    skip,
                    c * width,
                    width,
                    new_len,
                )
            )
        results.append(jnp.concatenate(pieces, axis=1))
    return jnp.concatenate(results, axis=0)


def solution(mesh):
    placed = (
        P(("groups", "tok"), "chan"),
        P(),
        P("tok", None, "chan"),
        P(None, None, "chan"),
        P("chan", None),
        P("chan"),
        P(("groups", "tok"), None, "chan"),
        P(("groups", "tok"), None, None, "chan"),
        P("groups"),
        P("groups"),
    )
    return jax.shard_map(
        on_device,
        mesh=mesh,
        in_specs=placed,
        out_specs=P(("groups", "tok"), "chan"),
        check_vma=False,
    )
```

time: 992 us -> 380 us (0.38)
  waiting for transfers between devices: 518 us -> 143 us
  local copies, waits for them, and re-layouts: 313 us -> 20.2 us
  other arithmetic: 75.9 us -> 20.6 us
  matrix products: 68.1 us -> 117 us
  Pallas kernels: 0 us -> 20.8 us
  starting transfers between devices: 0.12 us -> 20.5 us
  between operations: 13.3 us -> 30.4 us
    all_gather x4 -> x2, waiting for transfers between devices: 516 us -> 65.3 us  [on_device(): lax.all_gather(hidden[p * new_len:(p + 1) * new_len], 'chan', axis=1, til...]
    gather x5 -> x0, local copies, waits for them, and re-layouts: 185 us -> none  [the longest x2 176 us: long_filter(): table = jnp.take(filters, jnp.clip(lagged, 0, FILTER - 1), axis=1)]
    ppermute x0 -> x24, waiting for transfers between devices: none -> 78 us  [swap(): return lax.ppermute(value, 'tok', [(i, i ^ mask) for i in range(count)])]
    dot_general x2 -> x48, matrix products: 68.1 us -> 117 us  [the longest x24 58.7 us: on_device(): jnp.dot(keep, part[s], preferred_element_type=jnp.float32)]
    select_n x3 -> x0, local copies, waits for them, and re-layouts: 31.2 us -> none  [the longest x1 30.7 us: long_filter(): table = jnp.where(valid[None], table, jnp.float32(0.0))]
    unnamed x24, local copies, waits for them, and re-layouts: 40.5 us -> 10.8 us
    add x2 -> x8, other arithmetic: 30.4 us -> 2.82 us  [on_device(): now = held + back.astype(jnp.float32)]
    all_gather x2 -> x0, local copies, waits for them, and re-layouts: 24.5 us -> none  [the longest x1 20.6 us: on_device(): lax.all_gather(u_store, 'tok', axis=0, tiled=True)]
  transfers between devices with their start and end apart: 4 -> 26, of which waited for: 1 -> 13; matrix products, arithmetic and copies ran while one was open for 30% -> 28% of each run, Pallas kernels for 0% -> 5%
where the time goes in v1:
time: 380 us; the launch traced here: 373 us
  waiting for transfers between devices  143 us (38%)
  matrix products  117 us (31%)
  between operations  30.4 us (8%)
  Pallas kernels  20.8 us (5%)
  other arithmetic  20.6 us (5%)
  starting transfers between devices  20.5 us (5%)
  local copies, waits for them, and re-layouts  20.2 us (5%)
    ppermute x24, waiting for transfers between devices, swap(): return lax.ppermute(value, 'tok', [(i, i ^ mask) for i in range(count)])  78 us
    all_gather x2, waiting for transfers between devices, on_device(): lax.all_gather(hidden[p * new_len:(p + 1) * new_len], 'chan', axis=1, til...  65.3 us
    dot_general x24, matrix products, on_device(): jnp.dot(keep, part[s], preferred_element_type=jnp.float32)  58.7 us
    dot_general x24, matrix products, on_device(): jnp.dot(leave, part[s], preferred_element_type=jnp.float32)  58.7 us
    pallas_call x8, Pallas kernels, mix(): pl.pallas_call(body, grid=(width // tile,), out_shape=jax.ShapeDtypeStruc...  20.8 us
    ppermute x24, starting transfers between devices, swap(): return lax.ppermute(value, 'tok', [(i, i ^ mask) for i in range(count)])  20.5 us
    unnamed x24, local copies, waits for them, and re-layouts  10.8 us
  transfers between devices with their start and end apart: 26, of which 13 were waited for; matrix products, arithmetic and copies ran while one was open for 28% of the time, Pallas kernels for 5%

profile of v1, /device:TPU:0, one launch (start us, length us, event | category | flops | bytes accessed | tf_op | source)
XLA Modules:
  0.0 373.2 jit_solution(6158044551542209528)
XLA Ops:
  6.5 2.5 fusion.377
  20.8 6.5 %copy.12 = bf16[8,127,2048]{2,1,0:T(8,128)(2,1)} copy(bf16[8,127,2048]{2,0,1:T(8,128)(2,1)} %param.16) | data formatting | bytes 8323072 | tf_op args[6]
  42.4 4.6 %collective-permute-done.5 = bf16[2,2,176,2048]{3,2,1,0:T(8,128)(2,1)} collective-permute-done((bf16[2,2,176,2048]{3,2,1,0:T(8,128)(2,1)S(1)}, bf16[2,2,176,2048]{3,2,1,0:T(8,128)(2,1)}, u32[]{:S(2)}, u32[]{:S(2)}) %collective-permute-start.5) | collective-permute-done | bytes 2883616 | tf_op jit(solution)/shard_map/ppermute | solution.py:17
  47.1 3.1 slice_select_fusion
  51.4 2.9 collective-permute-start.6
  54.3 12.4 %all-gather.5.cloned.1.call-done = bf16[160,8192]{1,0:T(8,128)(2,1)} async-done(((bf16[160,2048]{1,0:T(8,128)(2,1)}), bf16[160,8192]{1,0:T(8,128)(2,1)}) %all-gather.5.cloned.1.call-update) | async-done | bytes 2621456 | tf_op jit(solution)/shard_map/all_gather | solution.py:147
  69.1 52.8 %all-gather.3.cloned.1.call-done = bf16[160,8192]{1,0:T(8,128)(2,1)} async-done(((bf16[160,2048]{1,0:T(8,128)(2,1)}), bf16[160,8192]{1,0:T(8,128)(2,1)}) %all-gather.3.cloned.1.call-update) | async-done | bytes 2621456 | tf_op jit(solution)/shard_map/all_gather | solution.py:147
  121.9 2.5 fusion
  124.4 3.3 fusion.2
  134.6 10.2 %collective-permute-done.2 = bf16[160,2048]{1,0:T(8,128)(2,1)S(1)} collective-permute-done((bf16[160,2048]{1,0:T(8,128)(2,1)S(1)}, bf16[160,2048]{1,0:T(8,128)(2,1)S(1)}, u32[]{:S(2)}, u32[]{:S(2)}) %collective-permute-start.2) | collective-permute-done | bytes 655392 | tf_op jit(solution)/shard_map/ppermute | solution.py:17
  144.8 2.4 fusion.349
  147.2 2.4 fusion.355
  152.1 7.7 %collective-permute-done = bf16[160,2048]{1,0:T(8,128)(2,1)S(1)} collective-permute-done((bf16[160,2048]{1,0:T(8,128)(2,1)S(1)}, bf16[160,2048]{1,0:T(8,128)(2,1)S(1)}, u32[]{:S(2)}, u32[]{:S(2)}) %collective-permute-start) | collective-permute-done | bytes 655392 | tf_op jit(solution)/shard_map/ppermute | solution.py:17
  159.9 2.4 fusion.151
  162.3 2.4 fusion.157
  164.8 2.4 fusion.163
  167.3 2.4 fusion.331
  169.7 2.4 fusion.337
  172.1 2.4 fusion.343
  174.6 2.5 fusion.169
  177.0 2.5 fusion.175
  179.5 2.5 fusion.181
  181.9 2.4 fusion.313
  184.4 2.4 fusion.319
  186.8 2.6 fusion.325
  189.4 2.4 fusion.187
  191.9 2.4 fusion.193
  194.3 2.4 fusion.199
  196.8 2.4 fusion.295
  204.1 2.4 fusion.205
  206.6 2.5 fusion.211
  209.1 2.4 fusion.217
  211.6 2.4 fusion.352
  219.0 2.4 fusion.154
  221.5 2.4 fusion.160
  223.9 2.4 fusion.166
  231.2 2.4 fusion.346
  233.7 2.4 fusion.172
  236.1 2.4 fusion.178
  238.6 2.4 fusion.184
  241.0 2.4 fusion.316
  245.9 2.7 fusion.328
  248.6 2.4 fusion.190
  251.0 2.4 fusion.196
  253.5 2.4 fusion.202
  258.4 2.4 fusion.304
  263.3 2.5 fusion.208
  267.6 2.4 fusion.214
  270.3 2.4 fusion.220
  283.9 5.4 %collective-permute-done.4 = bf16[3,1,160,512]{3,2,0,1:T(8,128)(2,1)S(1)} collective-permute-done((bf16[3,1,160,512]{3,2,0,1:T(8,128)(2,1)S(1)}, bf16[3,1,160,512]{3,2,0,1:T(8,128)(2,1)S(1)}, u32[]{:S(2)}, u32[]{:S(2)}) %collective-permute-start.4) | collective-permute-done | bytes 491552 | tf_op jit(solution)/shard_map/ppermute | solution.py:17
  290.8 9.1 %collective-permute-done.8 = bf16[3,1,160,512]{3,2,0,1:T(8,128)(2,1)S(1)} collective-permute-done((bf16[3,1,160,512]{3,2,0,1:T(8,128)(2,1)S(1)}, bf16[3,1,160,512]{3,2,0,1:T(8,128)(2,1)S(1)}, u32[]{:S(2)}, u32[]{:S(2)}) %collective-permute-start.8) | collective-permute-done | bytes 491552 | tf_op jit(solution)/shard_map/ppermute | solution.py:17
  301.5 9.0 %collective-permute-done.10 = bf16[3,1,160,512]{3,2,0,1:T(8,128)(2,1)S(1)} collective-permute-done((bf16[3,1,160,512]{3,2,0,1:T(8,128)(2,1)S(1)}, bf16[3,1,160,512]{3,2,0,1:T(8,128)(2,1)S(1)}, u32[]{:S(2)}, u32[]{:S(2)}) %collective-permute-start.10) | collective-permute-done | bytes 491552 | tf_op jit(solution)/shard_map/ppermute | solution.py:17
  311.9 2.5 shard_map.100
  314.4 2.9 shard_map.101
  317.3 2.6 shard_map.102
  321.0 2.6 shard_map.103
  323.6 7.9 %collective-permute-done.17 = bf16[3,1,160,512]{3,2,0,1:T(8,128)(2,1)S(1)} collective-permute-done((bf16[3,1,160,512]{3,2,0,1:T(8,128)(2,1)S(1)}, bf16[3,1,160,512]{3,2,0,1:T(8,128)(2,1)S(1)}, u32[]{:S(2)}, u32[]{:S(2)}) %collective-permute-start.17) | collective-permute-done | bytes 491552 | tf_op jit(solution)/shard_map/ppermute | solution.py:17
  331.5 2.6 shard_map.104
  334.1 8.0 %collective-permute-done.19 = bf16[3,1,160,512]{3,2,0,1:T(8,128)(2,1)S(1)} collective-permute-done((bf16[3,1,160,512]{3,2,0,1:T(8,128)(2,1)S(1)}, bf16[3,1,160,512]{3,2,0,1:T(8,128)(2,1)S(1)}, u32[]{:S(2)}, u32[]{:S(2)}) %collective-permute-start.19) | collective-permute-done | bytes 491552 | tf_op jit(solution)/shard_map/ppermute | solution.py:17
  342.0 2.6 shard_map.105
  344.6 8.0 %collective-permute-done.21 = bf16[3,1,160,512]{3,2,0,1:T(8,128)(2,1)S(1)} collective-permute-done((bf16[3,1,160,512]{3,2,0,1:T(8,128)(2,1)S(1)}, bf16[3,1,160,512]{3,2,0,1:T(8,128)(2,1)S(1)}, u32[]{:S(2)}, u32[]{:S(2)}) %collective-permute-start.21) | collective-permute-done | bytes 491552 | tf_op jit(solution)/shard_map/ppermute | solution.py:17
  352.6 2.6 shard_map.106
  355.2 7.0 %collective-permute-done.23 = bf16[3,1,160,512]{3,2,0,1:T(8,128)(2,1)S(1)} collective-permute-done((bf16[3,1,160,512]{3,2,0,1:T(8,128)(2,1)S(1)}, bf16[3,1,160,512]{3,2,0,1:T(8,128)(2,1)S(1)}, u32[]{:S(2)}, u32[]{:S(2)}) %collective-permute-start.23) | collective-permute-done | bytes 491552 | tf_op jit(solution)/shard_map/ppermute | solution.py:17
  362.2 2.5 shard_map.107
  (148 shorter events, 66.0 us)
Async XLA Ops:
  6.5 2.6 copy-start.8
  6.5 60.2 %all-gather.5.cloned.1.call-start = ((), (), s32[]{:S(2)}) async-start(), calls=%async_computation.1 | async-start | bytes 3276800 | tf_op jit(solution)/shard_map/all_gather | solution.py:147
  9.1 112.8 %all-gather.3.cloned.1.call-start = ((), (), s32[]{:S(2)}) async-start(), calls=%async_computation | async-start | bytes 3276800 | tf_op jit(solution)/shard_map/all_gather | solution.py:147
  20.8 6.5 %copy-start.5 = (bf16[8,6,3,2048]{3,0,2,1:T(8,128)(2,1)S(1)}, bf16[8,6,3,2048]{3,0,2,1:T(8,128)(2,1)}, u32[]{:S(2)}) copy-start(bf16[8,6,3,2048]{3,0,2,1:T(8,128)(2,1)} %param.17) | copy-start | bytes 1769476
  32.7 2.2 copy-start.3
  39.1 2.5 copy-start.2
  39.1 2.9 copy-start.7
  39.1 3.0 copy-start.9
  39.1 3.1 copy-start.6
  41.6 5.5 %collective-permute-start.5 = (bf16[2,2,176,2048]{3,2,1,0:T(8,128)(2,1)S(1)}, bf16[2,2,176,2048]{3,2,1,0:T(8,128)(2,1)}, u32[]{:S(2)}, u32[]{:S(2)}) collective-permute-start(bf16[2,2,176,2048]{3,2,1,0:T(8,128)(2,1)S(1)} %slice.269), channel_id=1, source_target_pairs={{0,1},{1,0},{2,3},{3,2},{4,5},{5,4},{6,7},{7,6},{8,9},{9,8},{10,11... | collective-permute-start | bytes 8650760 | tf_op jit(solution)/shard_map/ppermute | solution.py:17
  51.4 79.2 %collective-permute-start.6 = (bf16[1,2,176,2048]{3,2,1,0:T(8,128)(2,1)}, bf16[1,2,176,2048]{3,2,1,0:T(8,128)(2,1)}, u32[]{:S(2)}, u32[]{:S(2)}) collective-permute-start(bf16[1,2,176,2048]{3,2,1,0:T(8,128)(2,1)} %slice.306), channel_id=1, source_target_pairs={{0,2},{1,3},{2,0},{3,1},{4,6},{5,7},{6,4},{7,5},{8,10},{9,11},{10,... | collective-permute-start | bytes 4325384 | tf_op jit(solution)/shard_map/ppermute | solution.py:17
  121.9 2.5 copy-start.4
  128.0 5.9 %collective-permute-start.1 = (bf16[160,2048]{1,0:T(8,128)(2,1)S(1)}, bf16[160,2048]{1,0:T(8,128)(2,1)S(1)}, u32[]{:S(2)}, u32[]{:S(2)}) collective-permute-start(bf16[160,2048]{1,0:T(8,128)(2,1)S(1)} %get-tuple-element.14), channel_id=1, source_target_pairs={{0,1},{1,0},{2,3},{3,2},{4,5},{5,4},{6,7},{7,6},{8,9},{9,8},{10,11... | collective-permute-start | bytes 1966088 | tf_op jit(solution)/shard_map/ppermute | solution.py:17
  128.1 16.7 %collective-permute-start.2 = (bf16[160,2048]{1,0:T(8,128)(2,1)S(1)}, bf16[160,2048]{1,0:T(8,128)(2,1)S(1)}, u32[]{:S(2)}, u32[]{:S(2)}) collective-permute-start(bf16[160,2048]{1,0:T(8,128)(2,1)S(1)} %get-tuple-element.13), channel_id=1, source_target_pairs={{0,3},{1,2},{2,1},{3,0},{4,7},{5,6},{6,5},{7,4},{8,11},{9,10},{10,... | collective-permute-start | bytes 1966088 | tf_op jit(solution)/shard_map/ppermute | solution.py:17
  129.7 30.1 %collective-permute-start = (bf16[160,2048]{1,0:T(8,128)(2,1)S(1)}, bf16[160,2048]{1,0:T(8,128)(2,1)S(1)}, u32[]{:S(2)}, u32[]{:S(2)}) collective-permute-start(bf16[160,2048]{1,0:T(8,128)(2,1)S(1)} %get-tuple-element.15), channel_id=1, source_target_pairs={{0,2},{1,3},{2,0},{3,1},{4,6},{5,7},{6,4},{7,5},{8,10},{9,11},{10,... | collective-permute-start | bytes 1966088 | tf_op jit(solution)/shard_map/ppermute | solution.py:17
  130.5 76.1 %collective-permute-start.14 = (bf16[160,2048]{1,0:T(8,128)(2,1)S(1)}, bf16[160,2048]{1,0:T(8,128)(2,1)S(1)}, u32[]{:S(2)}, u32[]{:S(2)}) collective-permute-start(bf16[160,2048]{1,0:T(8,128)(2,1)S(1)} %get-tuple-element.18), channel_id=1, source_target_pairs={{0,1},{1,0},{2,3},{3,2},{4,5},{5,4},{6,7},{7,6},{8,9},{9,8},{10,11... | collective-permute-start | bytes 1966088 | tf_op jit(solution)/shard_map/ppermute | solution.py:17
  130.6 80.9 %collective-permute-start.15 = (bf16[160,2048]{1,0:T(8,128)(2,1)S(1)}, bf16[160,2048]{1,0:T(8,128)(2,1)S(1)}, u32[]{:S(2)}, u32[]{:S(2)}) collective-permute-start(bf16[160,2048]{1,0:T(8,128)(2,1)S(1)} %get-tuple-element.17), channel_id=1, source_target_pairs={{0,3},{1,2},{2,1},{3,0},{4,7},{5,6},{6,5},{7,4},{8,11},{9,10},{10,... | collective-permute-start | bytes 1966088 | tf_op jit(solution)/shard_map/ppermute | solution.py:17
  133.9 85.0 %collective-permute-start.13 = (bf16[160,2048]{1,0:T(8,128)(2,1)S(1)}, bf16[160,2048]{1,0:T(8,128)(2,1)S(1)}, u32[]{:S(2)}, u32[]{:S(2)}) collective-permute-start(bf16[160,2048]{1,0:T(8,128)(2,1)S(1)} %get-tuple-element.19), channel_id=1, source_target_pairs={{0,2},{1,3},{2,0},{3,1},{4,6},{5,7},{6,4},{7,5},{8,10},{9,11},{10,... | collective-permute-start | bytes 1966088 | tf_op jit(solution)/shard_map/ppermute | solution.py:17
  265.8 7.1 %collective-permute-start.3 = (bf16[3,320,512]{2,1,0:T(8,128)(2,1)S(1)}, bf16[3,320,512]{2,1,0:T(8,128)(2,1)S(1)}, u32[]{:S(2)}, u32[]{:S(2)}) collective-permute-start(bf16[3,320,512]{2,1,0:T(8,128)(2,1)S(1)} %pad_maximum_fusion.3), channel_id=1, source_target_pairs={{0,1},{1,0},{2,3},{3,2},{4,5},{5,4},{6,7},{7,6},{8,9},{9,8},{10,11... | collective-permute-start | bytes 2949128 | tf_op jit(solution)/shard_map/ppermute | solution.py:17
  266.0 7.8 %collective-permute-start.7 = (bf16[3,320,512]{2,1,0:T(8,128)(2,1)S(1)}, bf16[3,320,512]{2,1,0:T(8,128)(2,1)S(1)}, u32[]{:S(2)}, u32[]{:S(2)}) collective-permute-start(bf16[3,320,512]{2,1,0:T(8,128)(2,1)S(1)} %pad_maximum_fusion.4), channel_id=1, source_target_pairs={{0,1},{1,0},{2,3},{3,2},{4,5},{5,4},{6,7},{7,6},{8,9},{9,8},{10,11... | collective-permute-start | bytes 2949128 | tf_op jit(solution)/shard_map/ppermute | solution.py:17
  266.7 7.6 %collective-permute-start.9 = (bf16[3,320,512]{2,1,0:T(8,128)(2,1)S(1)}, bf16[3,320,512]{2,1,0:T(8,128)(2,1)S(1)}, u32[]{:S(2)}, u32[]{:S(2)}) collective-permute-start(bf16[3,320,512]{2,1,0:T(8,128)(2,1)S(1)} %pad_maximum_fusion.5), channel_id=1, source_target_pairs={{0,1},{1,0},{2,3},{3,2},{4,5},{5,4},{6,7},{7,6},{8,9},{9,8},{10,11... | collective-permute-start | bytes 2949128 | tf_op jit(solution)/shard_map/ppermute | solution.py:17
  266.9 8.3 %collective-permute-start.11 = (bf16[3,320,512]{2,1,0:T(8,128)(2,1)S(1)}, bf16[3,320,512]{2,1,0:T(8,128)(2,1)S(1)}, u32[]{:S(2)}, u32[]{:S(2)}) collective-permute-start(bf16[3,320,512]{2,1,0:T(8,128)(2,1)S(1)} %pad_maximum_fusion.6), channel_id=1, source_target_pairs={{0,1},{1,0},{2,3},{3,2},{4,5},{5,4},{6,7},{7,6},{8,9},{9,8},{10,11... | collective-permute-start | bytes 2949128 | tf_op jit(solution)/shard_map/ppermute | solution.py:17
  267.6 9.8 %collective-permute-start.16 = (bf16[3,320,512]{2,1,0:T(8,128)(2,1)S(1)}, bf16[3,320,512]{2,1,0:T(8,128)(2,1)S(1)}, u32[]{:S(2)}, u32[]{:S(2)}) collective-permute-start(bf16[3,320,512]{2,1,0:T(8,128)(2,1)S(1)} %pad_maximum_fusion.7), channel_id=1, source_target_pairs={{0,1},{1,0},{2,3},{3,2},{4,5},{5,4},{6,7},{7,6},{8,9},{9,8},{10,11... | collective-permute-start | bytes 2949128 | tf_op jit(solution)/shard_map/ppermute | solution.py:17
  272.9 5.5 %collective-permute-start.18 = (bf16[3,320,512]{2,1,0:T(8,128)(2,1)S(1)}, bf16[3,320,512]{2,1,0:T(8,128)(2,1)S(1)}, u32[]{:S(2)}, u32[]{:S(2)}) collective-permute-start(bf16[3,320,512]{2,1,0:T(8,128)(2,1)S(1)} %pad_maximum_fusion.8), channel_id=1, source_target_pairs={{0,1},{1,0},{2,3},{3,2},{4,5},{5,4},{6,7},{7,6},{8,9},{9,8},{10,11... | collective-permute-start | bytes 2949128 | tf_op jit(solution)/shard_map/ppermute | solution.py:17
  273.9 6.6 %collective-permute-start.20 = (bf16[3,320,512]{2,1,0:T(8,128)(2,1)S(1)}, bf16[3,320,512]{2,1,0:T(8,128)(2,1)S(1)}, u32[]{:S(2)}, u32[]{:S(2)}) collective-permute-start(bf16[3,320,512]{2,1,0:T(8,128)(2,1)S(1)} %pad_maximum_fusion.9), channel_id=1, source_target_pairs={{0,1},{1,0},{2,3},{3,2},{4,5},{5,4},{6,7},{7,6},{8,9},{9,8},{10,11... | collective-permute-start | bytes 2949128 | tf_op jit(solution)/shard_map/ppermute | solution.py:17
  274.3 7.5 %collective-permute-start.22 = (bf16[3,320,512]{2,1,0:T(8,128)(2,1)S(1)}, bf16[3,320,512]{2,1,0:T(8,128)(2,1)S(1)}, u32[]{:S(2)}, u32[]{:S(2)}) collective-permute-start(bf16[3,320,512]{2,1,0:T(8,128)(2,1)S(1)} %pad_maximum_fusion.10), channel_id=1, source_target_pairs={{0,1},{1,0},{2,3},{3,2},{4,5},{5,4},{6,7},{7,6},{8,9},{9,8},{10,11... | collective-permute-start | bytes 2949128 | tf_op jit(solution)/shard_map/ppermute | solution.py:17
  275.2 14.2 %collective-permute-start.4 = (bf16[3,1,160,512]{3,2,0,1:T(8,128)(2,1)S(1)}, bf16[3,1,160,512]{3,2,0,1:T(8,128)(2,1)S(1)}, u32[]{:S(2)}, u32[]{:S(2)}) collective-permute-start(bf16[3,1,160,512]{3,2,0,1:T(8,128)(2,1)S(1)} %slice.699), channel_id=1, source_target_pairs={{0,2},{1,3},{2,0},{3,1},{4,6},{5,7},{6,4},{7,5},{8,10},{9,11},{10,... | collective-permute-start | bytes 1474568 | tf_op jit(solution)/shard_map/ppermute | solution.py:17
  277.3 22.6 %collective-permute-start.8 = (bf16[3,1,160,512]{3,2,0,1:T(8,128)(2,1)S(1)}, bf16[3,1,160,512]{3,2,0,1:T(8,128)(2,1)S(1)}, u32[]{:S(2)}, u32[]{:S(2)}) collective-permute-start(bf16[3,1,160,512]{3,2,0,1:T(8,128)(2,1)S(1)} %slice.698), channel_id=1, source_target_pairs={{0,2},{1,3},{2,0},{3,1},{4,6},{5,7},{6,4},{7,5},{8,10},{9,11},{10,... | collective-permute-start | bytes 1474568 | tf_op jit(solution)/shard_map/ppermute | solution.py:17
  278.4 32.0 %collective-permute-start.10 = (bf16[3,1,160,512]{3,2,0,1:T(8,128)(2,1)S(1)}, bf16[3,1,160,512]{3,2,0,1:T(8,128)(2,1)S(1)}, u32[]{:S(2)}, u32[]{:S(2)}) collective-permute-start(bf16[3,1,160,512]{3,2,0,1:T(8,128)(2,1)S(1)} %slice.697), channel_id=1, source_target_pairs={{0,2},{1,3},{2,0},{3,1},{4,6},{5,7},{6,4},{7,5},{8,10},{9,11},{10,... | collective-permute-start | bytes 1474568 | tf_op jit(solution)/shard_map/ppermute | solution.py:17
  280.5 40.5 %collective-permute-start.12 = (bf16[3,1,160,512]{3,2,0,1:T(8,128)(2,1)S(1)}, bf16[3,1,160,512]{3,2,0,1:T(8,128)(2,1)S(1)}, u32[]{:S(2)}, u32[]{:S(2)}) collective-permute-start(bf16[3,1,160,512]{3,2,0,1:T(8,128)(2,1)S(1)} %slice.696), channel_id=1, source_target_pairs={{0,2},{1,3},{2,0},{3,1},{4,6},{5,7},{6,4},{7,5},{8,10},{9,11},{10,... | collective-permute-start | bytes 1474568 | tf_op jit(solution)/shard_map/ppermute | solution.py:17
  281.9 49.6 %collective-permute-start.17 = (bf16[3,1,160,512]{3,2,0,1:T(8,128)(2,1)S(1)}, bf16[3,1,160,512]{3,2,0,1:T(8,128)(2,1)S(1)}, u32[]{:S(2)}, u32[]{:S(2)}) collective-permute-start(bf16[3,1,160,512]{3,2,0,1:T(8,128)(2,1)S(1)} %slice.695), channel_id=1, source_target_pairs={{0,2},{1,3},{2,0},{3,1},{4,6},{5,7},{6,4},{7,5},{8,10},{9,11},{10,... | collective-permute-start | bytes 1474568 | tf_op jit(solution)/shard_map/ppermute | solution.py:17
  283.9 28.0 %copy-start = (f32[3,7,2048]{2,1,0:T(8,128)S(1)}, f32[3,7,2048]{2,1,0:T(8,128)}, u32[]{:S(2)}) copy-start(f32[3,7,2048]{2,1,0:T(8,128)} %refs_4_.15) | copy-start | bytes 516100
  283.9 28.0 %copy-start.1 = (f32[2048]{0:T(1024)S(1)}, f32[2048]{0:T(1024)}, u32[]{:S(2)}) copy-start(f32[2048]{0:T(1024)} %param.15) | copy-start | bytes 24580
  289.4 52.7 %collective-permute-start.19 = (bf16[3,1,160,512]{3,2,0,1:T(8,128)(2,1)S(1)}, bf16[3,1,160,512]{3,2,0,1:T(8,128)(2,1)S(1)}, u32[]{:S(2)}, u32[]{:S(2)}) collective-permute-start(bf16[3,1,160,512]{3,2,0,1:T(8,128)(2,1)S(1)} %slice.694), channel_id=1, source_target_pairs={{0,2},{1,3},{2,0},{3,1},{4,6},{5,7},{6,4},{7,5},{8,10},{9,11},{10,... | collective-permute-start | bytes 1474568 | tf_op jit(solution)/shard_map/ppermute | solution.py:17
  299.9 52.7 %collective-permute-start.21 = (bf16[3,1,160,512]{3,2,0,1:T(8,128)(2,1)S(1)}, bf16[3,1,160,512]{3,2,0,1:T(8,128)(2,1)S(1)}, u32[]{:S(2)}, u32[]{:S(2)}) collective-permute-start(bf16[3,1,160,512]{3,2,0,1:T(8,128)(2,1)S(1)} %slice.693), channel_id=1, source_target_pairs={{0,2},{1,3},{2,0},{3,1},{4,6},{5,7},{6,4},{7,5},{8,10},{9,11},{10,... | collective-permute-start | bytes 1474568 | tf_op jit(solution)/shard_map/ppermute | solution.py:17
  310.4 51.7 %collective-permute-start.23 = (bf16[3,1,160,512]{3,2,0,1:T(8,128)(2,1)S(1)}, bf16[3,1,160,512]{3,2,0,1:T(8,128)(2,1)S(1)}, u32[]{:S(2)}, u32[]{:S(2)}) collective-permute-start(bf16[3,1,160,512]{3,2,0,1:T(8,128)(2,1)S(1)} %slice.692), channel_id=1, source_target_pairs={{0,2},{1,3},{2,0},{3,1},{4,6},{5,7},{6,4},{7,5},{8,10},{9,11},{10,... | collective-permute-start | bytes 1474568 | tf_op jit(solution)/shard_map/ppermute | solution.py:17
Sparse Core Ops, SparseCore 0:
  9.2 57.4 all-gather.4
  68.3 53.5 all-gather.2

commit v2 on v1

--- a/solution.py
+++ b/solution.py
@@ -27,9 +27,9 @@
 
     def short(p, s):
         rows = pl.ds(p * new_len, new_len)
-        total = parts[0][s, rows, :].astype(jnp.float32)
+        total = parts[0][s, 0, rows, :].astype(jnp.float32)
         for part in parts[1:]:
-            total = total + part[s, rows, :].astype(jnp.float32)
+            total = total + part[s, 0, rows, :].astype(jnp.float32)
         z_scr[0:PAD, :] = z_ref[p, s * PAD : (s + 1) * PAD, :].astype(jnp.float32)
         z_scr[PAD : PAD + new_len, :] = total.astype(jnp.bfloat16).astype(jnp.float32)
         acc = taps_ref[s, 0:1, :] * z_scr[PAD : PAD + new_len, :]
@@ -56,8 +56,44 @@
         out_ref[p * new_len : (p + 1) * new_len, :] = (short(p, 0) * mixed).astype(jnp.bfloat16)
 
 
+def project_kernel(x_ref, w_ref, sent_ref, kept_ref):
+    half = sent_ref.shape[1]
+    sent_ref[0] = jnp.dot(
+        x_ref[0:half, :], w_ref[0], preferred_element_type=jnp.float32
+    ).astype(jnp.bfloat16)
+    kept_ref[0] = jnp.dot(x_ref[half:, :], w_ref[0], preferred_element_type=jnp.float32)
+
+
+def project(x, weights, base, width):
+    rows, depth = x.shape
+    half = rows // 2
+    off = base // width
+    return pl.pallas_call(
+        project_kernel,
+        grid=(3,),
+        out_shape=(
+            jax.ShapeDtypeStruct((3, half, width), jnp.bfloat16),
+            jax.ShapeDtypeStruct((3, half, width), jnp.float32),
+        ),
+        in_specs=[
+            pl.BlockSpec((rows, depth), lambda i: (0, 0)),
+            pl.BlockSpec((1, depth, width), lambda i: (i, 0, off)),
+        ],
+        out_specs=(
+            pl.BlockSpec((1, half, width), lambda i: (i, 0, 0)),
+            pl.BlockSpec((1, half, width), lambda i: (i, 0, 0)),
+        ),
+        compiler_params=pltpu.CompilerParams(vmem_limit_bytes=40 * 1024 * 1024),
+        cost_estimate=pl.CostEstimate(
+            flops=6 * rows * depth * width,
+            bytes_accessed=6 * depth * width + 2 * rows * depth + 9 * rows * width,
+            transcendentals=0,
+        ),
+    )(x, weights)
+
+
 def mix(parts, z_tail, u_tail, taps, filters, skip, base, width, new_len):
-    rows = parts[0].shape[1]
+    rows = parts[0].shape[2]
     prompts = z_tail.shape[0]
     tile = min(256, width)
     off = base // tile
@@ -66,7 +102,7 @@
         body,
         grid=(width // tile,),
         out_shape=jax.ShapeDtypeStruct((rows, width), jnp.bfloat16),
-        in_specs=[pl.BlockSpec((3, rows, tile), lambda i: (0, 0, i)) for _ in parts]
+        in_specs=[pl.BlockSpec((3, 1, rows, tile), lambda i: (0, 0, 0, i)) for _ in parts]
         + [
             pl.BlockSpec((prompts, 3 * PAD, tile), lambda i: (0, 0, i + off)),
             pl.BlockSpec((prompts, FILTER, tile), lambda i: (0, 0, i + off)),
@@ -113,15 +149,17 @@
     keys = jnp.stack(keys)
     held = jnp.stack(blocks)
     bit = 0
+    begun = held
     while (1 << bit) < count:
         mask = 1 << bit
+        begun = held
         got = swap(held[1::2], count, mask)
         keys = keys[0::2]
         take = (keys >> bit) == ((me ^ mask) >> bit)
         held = jnp.where(take[:, :, None, None], got, held[0::2])
         bit += 1
     held = held[0]
-    return held[:, 0:FILTER], held[:, FILTER:]
+    return held[:, 0:FILTER], held[:, FILTER:], begun
 
 
 def on_device(
@@ -134,7 +172,7 @@
     me = lax.axis_index("tok")
     per_shard = holder.shape[0] // count
     new_len = rows // per_shard
-    u_tail, z_tail = tails(u_store, z_store, holder, slot, count, per_shard)
+    u_tail, z_tail, begun = tails(u_store, z_store, holder, slot, count, per_shard)
     weights = jnp.transpose(w_in, (1, 0, 2))
     filters = jnp.pad(mr_filter[:, ::-1], ((0, 0), (1, FILTER - 1)))
     skip = skip_gain.reshape(1, chans)
@@ -148,37 +186,41 @@
         for p in range(per_shard)
     ]
     results = []
+    after = begun
+    landed = []
     for p in range(per_shard):
-        values = wholes[p].astype(jnp.float32)
+        whole = wholes[p]
+        whole, _ = lax.optimization_barrier((whole, after))
+        values = whole.astype(jnp.float32)
         meansq = jnp.mean(values * values, axis=-1, keepdims=True)
         normed = (values * lax.rsqrt(meansq + 1e-06) * gain).astype(jnp.bfloat16)
         got = {}
         for s in range(count):
             mine = lax.dynamic_slice_in_dim(normed, (me ^ s) * depth, depth, 1)
             got[s] = mine if s == 0 else swap(mine, count, s)
-        leave = jnp.concatenate([got[s] for s in order[:half]], axis=0)
-        keep = jnp.concatenate([got[s] for s in order[half:]], axis=0)
+        rows_in = jnp.concatenate([got[s] for s in order], axis=0)
+        if results:
+            rows_in, _ = lax.optimization_barrier((rows_in, results[-1][:-1]))
         pieces = []
         for c in range(chunks):
-            part = weights[:, :, c * width : (c + 1) * width]
-            sent = jnp.stack(
-                [jnp.dot(leave, part[s], preferred_element_type=jnp.float32) for s in range(3)]
-            ).astype(jnp.bfloat16)
-            kept = jnp.stack(
-                [jnp.dot(keep, part[s], preferred_element_type=jnp.float32) for s in range(3)]
-            )
-            held = kept.reshape(3, half, new_len, width)
+            if len(landed) >= 3:
+                rows_in, _ = lax.optimization_barrier((rows_in, landed[-3]))
+            sent, kept = project(rows_in, weights, c * width, width)
+            after = kept
+            kept = kept.reshape(3, half, new_len, width)
             back = swap(sent, count, 1).reshape(3, half, new_len, width)
+            parts, now = [kept, back], [kept, back]
             bit = 1
             while (1 << bit) < count:
-                now = held + back.astype(jnp.float32)
-                out = now[:, 1::2].astype(jnp.bfloat16)
-                held = now[:, 0::2]
+                out = sum(part[:, 1::2].astype(jnp.float32) for part in now).astype(jnp.bfloat16)
                 back = swap(out, count, 1 << bit)
+                now = [part[:, 0::2] for part in now] + [back]
+                parts.append(back)
                 bit += 1
+            landed.append(back)
             pieces.append(
                 mix(
-                    [held[:, 0], back[:, 0]],
+                    parts,
                     z_tail[p : p + 1],
                     u_tail[p : p + 1],
                     short_taps,
@@ -189,8 +231,8 @@
                     new_len,
                 )
             )
-        results.append(jnp.concatenate(pieces, axis=1))
-    return jnp.concatenate(results, axis=0)
+        results.append(pieces)
+    return jnp.concatenate([jnp.concatenate(line, axis=1) for line in results], axis=0)
 
 
 def solution(mesh):

time: 380 us -> 283 us (0.74); the launches traced: 373 us -> 283 us
  matrix products: 117 us -> 0 us
  Pallas kernels: 20.8 us -> 74.6 us
  waiting for transfers between devices: 143 us -> 116 us
    dot_general x48 -> x0, matrix products: 117 us -> none  [the longest x24 58.7 us: on_device(): jnp.dot(keep, part[s], preferred_element_type=jnp.float32)]
    all_gather x2, waiting for transfers between devices: 65.3 us -> 12.5 us  [on_device(): lax.all_gather(hidden[p * new_len:(p + 1) * new_len], 'chan', axis=1, til...]
    pallas_call x0 -> x8, Pallas kernels: none -> 51.1 us  [project(): pl.pallas_call(project_kernel, grid=(3,), out_shape=(jax.ShapeDtypeStruct...]
    ppermute x24, waiting for transfers between devices: 78 us -> 103 us  [swap(): return lax.ppermute(value, 'tok', [(i, i ^ mask) for i in range(count)])]
    unnamed x24 -> x58, local copies, waits for them, and re-layouts: 10.8 us -> 10.8 us
  transfers between devices with their start and end apart: 26 -> 26, of which waited for: 13 -> 15; matrix products, arithmetic and copies ran while one was open for 28% -> 13% of each run, Pallas kernels for 5% -> 25%
where the time goes in v2:
time: 283 us
  waiting for transfers between devices  116 us (41%)
  Pallas kernels  74.6 us (26%)
  between operations  29.4 us (10%)
  local copies, waits for them, and re-layouts  23.6 us (8%)
  other arithmetic  19.8 us (7%)
  starting transfers between devices  19.6 us (7%)
    ppermute x24, waiting for transfers between devices, swap(): return lax.ppermute(value, 'tok', [(i, i ^ mask) for i in range(count)])  103 us
    pallas_call x8, Pallas kernels, project(): pl.pallas_call(project_kernel, grid=(3,), out_shape=(jax.ShapeDtypeStruct...  51.1 us
    pallas_call x8, Pallas kernels, mix(): pl.pallas_call(body, grid=(width // tile,), out_shape=jax.ShapeDtypeStruc...  23.5 us
    ppermute x24, starting transfers between devices, swap(): return lax.ppermute(value, 'tok', [(i, i ^ mask) for i in range(count)])  19.6 us
    all_gather x2, waiting for transfers between devices, on_device(): lax.all_gather(hidden[p * new_len:(p + 1) * new_len], 'chan', axis=1, til...  12.5 us
    unnamed x58, local copies, waits for them, and re-layouts  10.8 us
  transfers between devices with their start and end apart: 26, of which 15 were waited for; matrix products, arithmetic and copies ran while one was open for 13% of the time, Pallas kernels for 25%

profile of v2, /device:TPU:0, one launch (start us, length us, event | category | flops | bytes accessed | tf_op | source)
XLA Modules:
  0.0 282.5 jit_solution(2591427964729007807)
XLA Ops:
  6.5 2.5 fusion.25
  9.3 0.7 fusion.26
  15.1 0.6 fusion.29
  20.7 6.6 %copy.11 = bf16[8,127,2048]{2,1,0:T(8,128)(2,1)} copy(bf16[8,127,2048]{2,0,1:T(8,128)(2,1)} %param.16) | data formatting | bytes 8323072 | tf_op args[6]
  33.0 3.6 %fusion.15 = (bf16[128,2048]{1,0:T(8,128)(2,1)S(1)}, bf16[128,2048]{1,0:T(8,128)(2,1)S(1)}, bf16[128,2048]{1,0:T(8,128)(2,1)S(1)}, bf16[128,2048]{1,0:T(8,128)(2...) fusion(s32[]{:T(128)S(6)} %select_n.78, ...), kind=kLoop, calls=%fused_computation.54 | loop fusion | bytes 8355872 | tf_op jit(solution)/shard_map/jit(dynamic_index_in_dim)/squeeze | solution.py:141
  37.8 1.4 pad_maximum_fusion
  39.7 2.0 copy-done.18
  41.7 0.4 collective-permute-start
  42.3 4.8 %collective-permute-done = bf16[2,2,176,2048]{3,2,1,0:T(8,128)(2,1)} collective-permute-done((bf16[2,2,176,2048]{3,2,1,0:T(8,128)(2,1)S(1)}, bf16[2,2,176,2048]{3,2,1,0:T(8,128)(2,1)}, u32[]{:S(2)}, u32[]{:S(2)}) %collective-permute-start) | collective-permute-done | bytes 2883616 | tf_op jit(solution)/shard_map/ppermute | solution.py:17
  47.1 3.1 %slice_select_fusion = bf16[2,2,176,2048]{3,2,1,0:T(8,128)(2,1)S(1)} fusion(bf16[2,2,176,2048]{3,2,1,0:T(8,128)(2,1)} %collective-permute-done, bf16[4,2,176,2048]{3,2,1,0:T(8,128)(2,1)} %copy-done.18, pred[2,2]{1,0:T(4,128)(4,1)S(1)} %shift-right-arithmetic_compare_fusion), kind=kLoop, calls=%fused_computation.11 | loop fusion | flops 1441792 | bytes 8650756 | tf_op jit(solution)/shard_map/jit(_where)/select_n | solution.py:159
  50.2 1.2 slice.191
  51.4 2.9 %collective-permute-start.6 = (bf16[1,2,176,2048]{3,2,1,0:T(8,128)(2,1)}, bf16[1,2,176,2048]{3,2,1,0:T(8,128)(2,1)}, u32[]{:S(2)}, u32[]{:S(2)}) collective-permute-start(bf16[1,2,176,2048]{3,2,1,0:T(8,128)(2,1)} %slice.191), channel_id=1, source_target_pairs={{0,2},{1,3},{2,0},{3,1},{4,6},{5,7},{6,4},{7,5},{8,10},{9,11},{10,... | collective-permute-start | bytes 4325384 | tf_op jit(solution)/shard_map/ppermute | solution.py:17
  54.3 12.4 %all-gather.3.cloned.1.call-done = bf16[160,8192]{1,0:T(8,128)(2,1)} async-done(((bf16[160,2048]{1,0:T(8,128)(2,1)}), bf16[160,8192]{1,0:T(8,128)(2,1)}) %all-gather.3.cloned.1.call-update) | async-done | bytes 2621456 | tf_op jit(solution)/shard_map/all_gather | solution.py:185
  66.7 2.5 fusion
  69.3 0.7 fusion.2
  70.0 1.5 constant_dynamic-slice_fusion.7
  71.6 1.6 collective-permute-start.2
  73.1 0.6 collective-permute-start.3
  73.9 13.1 %collective-permute-done.6 = bf16[1,2,176,2048]{3,2,1,0:T(8,128)(2,1)} collective-permute-done((bf16[1,2,176,2048]{3,2,1,0:T(8,128)(2,1)}, bf16[1,2,176,2048]{3,2,1,0:T(8,128)(2,1)}, u32[]{:S(2)}, u32[]{:S(2)}) %collective-permute-start.6) | collective-permute-done | bytes 1441824 | tf_op jit(solution)/shard_map/ppermute | solution.py:17
  87.0 1.6 fusion.6
  88.6 12.0 %collective-permute-done.2 = bf16[160,2048]{1,0:T(8,128)(2,1)} collective-permute-done((bf16[160,2048]{1,0:T(8,128)(2,1)}, bf16[160,2048]{1,0:T(8,128)(2,1)}, u32[]{:S(2)}, u32[]{:S(2)}) %collective-permute-start.2) | collective-permute-done | bytes 655392 | tf_op jit(solution)/shard_map/ppermute | solution.py:17
  100.6 14.0 %collective-permute-done.3 = bf16[160,2048]{1,0:T(8,128)(2,1)} collective-permute-done((bf16[160,2048]{1,0:T(8,128)(2,1)}, bf16[160,2048]{1,0:T(8,128)(2,1)}, u32[]{:S(2)}, u32[]{:S(2)}) %collective-permute-start.3) | collective-permute-done | bytes 655392 | tf_op jit(solution)/shard_map/ppermute | solution.py:17
  114.6 1.6 pad_maximum_fusion.1.x_ref
  116.2 6.2 %shard_map.100 = (bf16[3,320,512]{2,1,0:T(8,128)(2,1)S(1)}, f32[3,320,512]{2,1,0:T(8,128)S(1)}) custom-call(bf16[640,2048]{1,0:T(8,128)(2,1)S(1)} %pad_maximum_fusion.1.x_ref, bf16[3,2048,2048]{2,1,0:T(8,128)(2,1)} %bitcast.138), custom_call_target="tpu_custom_call" | custom-call | flops 4026531840 | bytes 11862016 | tf_op jit(solution)/shard_map/pallas_call | solution.py:71
  122.6 6.9 %shard_map.104 = (bf16[3,320,512]{2,1,0:T(8,128)(2,1)S(1)}, f32[3,320,512]{2,1,0:T(8,128)S(1)}) custom-call(bf16[640,2048]{1,0:T(8,128)(2,1)S(1)} %pad_maximum_fusion.1.x_ref, bf16[3,2048,2048]{2,1,0:T(8,128)(2,1)} %bitcast.139), custom_call_target="tpu_custom_call" | custom-call | flops 4026531840 | bytes 11862016 | tf_op jit(solution)/shard_map/pallas_call | solution.py:71
  129.5 6.9 %shard_map.102 = (bf16[3,320,512]{2,1,0:T(8,128)(2,1)S(1)}, f32[3,320,512]{2,1,0:T(8,128)S(1)}) custom-call(bf16[640,2048]{1,0:T(8,128)(2,1)S(1)} %pad_maximum_fusion.1.x_ref, bf16[3,2048,2048]{2,1,0:T(8,128)(2,1)} %bitcast.140), custom_call_target="tpu_custom_call" | custom-call | flops 4026531840 | bytes 11862016 | tf_op jit(solution)/shard_map/pallas_call | solution.py:71
  136.8 1.8 collective-permute-start.5
  138.6 1.1 fusion.12
  139.7 0.5 collective-permute-start.10
  140.2 1.1 fusion.13
  141.2 1.6 collective-permute-start.8
  142.8 8.1 %collective-permute-done.5.refs_2_ = bf16[3,1,160,512]{3,2,1,0:T(8,128)(2,1)S(1)} collective-permute-done((bf16[3,1,160,512]{3,2,1,0:T(8,128)(2,1)S(1)}, bf16[3,1,160,512]{3,2,1,0:T(8,128)(2,1)S(1)}, u32[]{:S(2)}, u32[]{:S(2)}) %collective-permute-start.5) | collective-permute-done | bytes 491552 | tf_op jit(solution)/shard_map/ppermute | solution.py:17
  150.9 0.8 copy-done.14
  151.6 6.2 %shard_map.106 = (bf16[3,320,512]{2,1,0:T(8,128)(2,1)S(1)}, f32[3,320,512]{2,1,0:T(8,128)S(1)}) custom-call(bf16[640,2048]{1,0:T(8,128)(2,1)S(1)} %pad_maximum_fusion.1.x_ref, bf16[3,2048,2048]{2,1,0:T(8,128)(2,1)} %bitcast.141), custom_call_target="tpu_custom_call" | custom-call | flops 4026531840 | bytes 11862016 | tf_op jit(solution)/shard_map/pallas_call | solution.py:71
  157.9 0.9 copy-done.16
  158.8 2.5 fusion.3
  161.3 0.7 fusion.5
  162.4 1.9 collective-permute-start.14
  164.6 1.2 fusion.24
  165.8 2.7 shard_map.101
  168.6 3.9 %shard_map.105 = bf16[160,512]{1,0:T(8,128)(2,1)S(1)} custom-call(f32[3,2,160,512]{3,2,1,0:T(8,128)S(1)} %bitcast.103, bf16[3,2,160,512]{3,2,1,0:T(8,128)(2,1)S(1)} %bitcast.119, bf16[3,1,160,512]{3,2,1,0:T(8,128)(2,1)} %collective-permute-done.10.refs_2_, bf16[1,48,2048]{2,1,0:T(8,128)(2,1)S(1)} %get-tuple-element.80.refs_3_, ...), custom_call_target="tpu_custom_call" | custom-call | flops 838860800 | bytes 2621440 | tf_op jit(solution)/shard_map/pallas_call | solution.py:101
  172.6 3.5 %shard_map.103 = bf16[160,512]{1,0:T(8,128)(2,1)S(1)} custom-call(f32[3,2,160,512]{3,2,1,0:T(8,128)S(1)} %bitcast.101, bf16[3,2,160,512]{3,2,1,0:T(8,128)(2,1)S(1)} %bitcast.117, bf16[3,1,160,512]{3,2,1,0:T(8,128)(2,1)} %collective-permute-done.8.refs_2_, bf16[1,48,2048]{2,1,0:T(8,128)(2,1)S(1)} %get-tuple-element.80.refs_3_, ...), custom_call_target="tpu_custom_call" | custom-call | flops 838860800 | bytes 2621440 | tf_op jit(solution)/shard_map/pallas_call | solution.py:101
  176.1 9.1 %collective-permute-done.14 = bf16[160,2048]{1,0:T(8,128)(2,1)S(1)} collective-permute-done((bf16[160,2048]{1,0:T(8,128)(2,1)S(1)}, bf16[160,2048]{1,0:T(8,128)(2,1)S(1)}, u32[]{:S(2)}, u32[]{:S(2)}) %collective-permute-start.14) | collective-permute-done | bytes 655392 | tf_op jit(solution)/shard_map/ppermute | solution.py:17
  185.2 14.4 %collective-permute-done.15 = bf16[160,2048]{1,0:T(8,128)(2,1)S(1)} collective-permute-done((bf16[160,2048]{1,0:T(8,128)(2,1)S(1)}, bf16[160,2048]{1,0:T(8,128)(2,1)S(1)}, u32[]{:S(2)}, u32[]{:S(2)}) %collective-permute-start.15) | collective-permute-done | bytes 655392 | tf_op jit(solution)/shard_map/ppermute | solution.py:17
  199.8 6.2 %shard_map.108 = (bf16[3,320,512]{2,1,0:T(8,128)(2,1)S(1)}, f32[3,320,512]{2,1,0:T(8,128)S(1)}) custom-call(bf16[640,2048]{1,0:T(8,128)(2,1)S(1)} %pad_maximum_fusion.2.x_ref, bf16[3,2048,2048]{2,1,0:T(8,128)(2,1)} %bitcast.142), custom_call_target="tpu_custom_call" | custom-call | flops 4026531840 | bytes 11862016 | tf_op jit(solution)/shard_map/pallas_call | solution.py:71
  206.3 1.8 collective-permute-start.12
  208.1 0.6 collective-permute-done.16
  208.9 1.8 collective-permute-start.17
  210.7 6.2 %shard_map.110 = (bf16[3,320,512]{2,1,0:T(8,128)(2,1)S(1)}, f32[3,320,512]{2,1,0:T(8,128)S(1)}) custom-call(bf16[640,2048]{1,0:T(8,128)(2,1)S(1)} %pad_maximum_fusion.2.x_ref, bf16[3,2048,2048]{2,1,0:T(8,128)(2,1)} %bitcast.143), custom_call_target="tpu_custom_call" | custom-call | flops 4026531840 | bytes 11862016 | tf_op jit(solution)/shard_map/pallas_call | solution.py:71
  217.0 3.4 %collective-permute-done.12.refs_2_ = bf16[3,1,160,512]{3,2,1,0:T(8,128)(2,1)S(1)} collective-permute-done((bf16[3,1,160,512]{3,2,1,0:T(8,128)(2,1)S(1)}, bf16[3,1,160,512]{3,2,1,0:T(8,128)(2,1)S(1)}, u32[]{:S(2)}, u32[]{:S(2)}) %collective-permute-start.12) | collective-permute-done | bytes 491552 | tf_op jit(solution)/shard_map/ppermute | solution.py:17
  220.4 6.2 %shard_map.112 = (bf16[3,320,512]{2,1,0:T(8,128)(2,1)S(1)}, f32[3,320,512]{2,1,0:T(8,128)S(1)}) custom-call(bf16[640,2048]{1,0:T(8,128)(2,1)S(1)} %pad_maximum_fusion.2.x_ref, bf16[3,2048,2048]{2,1,0:T(8,128)(2,1)} %bitcast.144), custom_call_target="tpu_custom_call" | custom-call | flops 4026531840 | bytes 11862016 | tf_op jit(solution)/shard_map/pallas_call | solution.py:71
  226.7 3.8 %collective-permute-done.17.refs_2_ = bf16[3,1,160,512]{3,2,1,0:T(8,128)(2,1)S(1)} collective-permute-done((bf16[3,1,160,512]{3,2,1,0:T(8,128)(2,1)S(1)}, bf16[3,1,160,512]{3,2,1,0:T(8,128)(2,1)S(1)}, u32[]{:S(2)}, u32[]{:S(2)}) %collective-permute-start.17) | collective-permute-done | bytes 491552 | tf_op jit(solution)/shard_map/ppermute | solution.py:17
  230.5 6.2 %shard_map.114 = (bf16[3,320,512]{2,1,0:T(8,128)(2,1)S(1)}, f32[3,320,512]{2,1,0:T(8,128)S(1)}) custom-call(bf16[640,2048]{1,0:T(8,128)(2,1)S(1)} %pad_maximum_fusion.2.x_ref, bf16[3,2048,2048]{2,1,0:T(8,128)(2,1)} %bitcast.145), custom_call_target="tpu_custom_call" | custom-call | flops 4026531840 | bytes 11862016 | tf_op jit(solution)/shard_map/pallas_call | solution.py:71
  237.0 1.8 collective-permute-start.19
  239.6 1.8 collective-permute-start.23
  241.4 2.7 shard_map.107
  244.0 2.7 shard_map.109
  246.7 4.4 %collective-permute-done.19.refs_2_ = bf16[3,1,160,512]{3,2,1,0:T(8,128)(2,1)S(1)} collective-permute-done((bf16[3,1,160,512]{3,2,1,0:T(8,128)(2,1)S(1)}, bf16[3,1,160,512]{3,2,1,0:T(8,128)(2,1)S(1)}, u32[]{:S(2)}, u32[]{:S(2)}) %collective-permute-start.19) | collective-permute-done | bytes 491552 | tf_op jit(solution)/shard_map/ppermute | solution.py:17
  251.1 2.7 shard_map.111
  253.8 7.9 %collective-permute-done.21.refs_2_ = bf16[3,1,160,512]{3,2,1,0:T(8,128)(2,1)S(1)} collective-permute-done((bf16[3,1,160,512]{3,2,1,0:T(8,128)(2,1)S(1)}, bf16[3,1,160,512]{3,2,1,0:T(8,128)(2,1)S(1)}, u32[]{:S(2)}, u32[]{:S(2)}) %collective-permute-start.21) | collective-permute-done | bytes 491552 | tf_op jit(solution)/shard_map/ppermute | solution.py:17
  261.6 2.7 shard_map.113
  264.4 7.4 %collective-permute-done.23.refs_2_ = bf16[3,1,160,512]{3,2,1,0:T(8,128)(2,1)S(1)} collective-permute-done((bf16[3,1,160,512]{3,2,1,0:T(8,128)(2,1)S(1)}, bf16[3,1,160,512]{3,2,1,0:T(8,128)(2,1)S(1)}, u32[]{:S(2)}, u32[]{:S(2)}) %collective-permute-start.23) | collective-permute-done | bytes 491552 | tf_op jit(solution)/shard_map/ppermute | solution.py:17
  271.8 2.7 shard_map.115
  274.5 1.2 maximum_maximum_fusion
  (117 shorter events, 5.5 us)
Async XLA Ops:
  6.5 2.7 copy-start.26
  6.5 60.2 %all-gather.3.cloned.1.call-start = ((), (), s32[]{:S(2)}) async-start(), calls=%async_computation | async-start | bytes 3276800 | tf_op jit(solution)/shard_map/all_gather | solution.py:185
  9.1 149.7 %all-gather.5.cloned.1.call-start = ((), (), s32[]{:S(2)}) async-start(), calls=%async_computation.1 | async-start | bytes 3276800 | tf_op jit(solution)/shard_map/all_gather | solution.py:185
  20.7 6.6 %copy-start.23 = (bf16[8,6,3,2048]{3,0,2,1:T(8,128)(2,1)S(1)}, bf16[8,6,3,2048]{3,0,2,1:T(8,128)(2,1)}, u32[]{:S(2)}) copy-start(bf16[8,6,3,2048]{3,0,2,1:T(8,128)(2,1)} %param.17) | copy-start | bytes 1769476
  39.3 2.4 copy-start.18
  39.3 2.9 %copy-start.27 = (s32[8]{0:T(128)S(1)}, s32[8]{0:T(128)}, u32[]{:S(2)}) copy-start(s32[8]{0:T(128)} %param.18) | copy-start | bytes 100
  39.3 3.0 %copy-start.25 = (bf16[8192]{0:T(1024)(128)(2,1)S(1)}, bf16[8192]{0:T(1024)(128)(2,1)}, u32[]{:S(2)}) copy-start(bf16[8192]{0:T(1024)(128)(2,1)} %param.11) | copy-start | bytes 49156
  41.7 5.4 %collective-permute-start = (bf16[2,2,176,2048]{3,2,1,0:T(8,128)(2,1)S(1)}, bf16[2,2,176,2048]{3,2,1,0:T(8,128)(2,1)}, u32[]{:S(2)}, u32[]{:S(2)}) collective-permute-start(bf16[2,2,176,2048]{3,2,1,0:T(8,128)(2,1)S(1)} %slice.163), channel_id=1, source_target_pairs={{0,1},{1,0},{2,3},{3,2},{4,5},{5,4},{6,7},{7,6},{8,9},{9,8},{10,11... | collective-permute-start | bytes 8650760 | tf_op jit(solution)/shard_map/ppermute | solution.py:17
  51.4 35.6 %collective-permute-start.6 = (bf16[1,2,176,2048]{3,2,1,0:T(8,128)(2,1)}, bf16[1,2,176,2048]{3,2,1,0:T(8,128)(2,1)}, u32[]{:S(2)}, u32[]{:S(2)}) collective-permute-start(bf16[1,2,176,2048]{3,2,1,0:T(8,128)(2,1)} %slice.191), channel_id=1, source_target_pairs={{0,2},{1,3},{2,0},{3,1},{4,6},{5,7},{6,4},{7,5},{8,10},{9,11},{10,... | collective-permute-start | bytes 4325384 | tf_op jit(solution)/shard_map/ppermute | solution.py:17
  66.7 2.5 copy-start.19
  70.0 3.7 %copy-start.24 = (f32[128,128]{1,0:T(8,128)S(1)}, f32[128,128]{1,0:T(8,128)}, u32[]{:S(2)}) copy-start(f32[128,128]{1,0:T(8,128)} %param.14) | copy-start | bytes 196612
  71.6 17.0 %collective-permute-start.1 = (bf16[160,2048]{1,0:T(8,128)(2,1)}, bf16[160,2048]{1,0:T(8,128)(2,1)}, u32[]{:S(2)}, u32[]{:S(2)}) collective-permute-start(bf16[160,2048]{1,0:T(8,128)(2,1)} %get-tuple-element.65), channel_id=1, source_target_pairs={{0,1},{1,0},{2,3},{3,2},{4,5},{5,4},{6,7},{7,6},{8,9},{9,8},{10,11... | collective-permute-start | bytes 1966088 | tf_op jit(solution)/shard_map/ppermute | solution.py:17
  71.6 29.0 %collective-permute-start.2 = (bf16[160,2048]{1,0:T(8,128)(2,1)}, bf16[160,2048]{1,0:T(8,128)(2,1)}, u32[]{:S(2)}, u32[]{:S(2)}) collective-permute-start(bf16[160,2048]{1,0:T(8,128)(2,1)} %get-tuple-element.68), channel_id=1, source_target_pairs={{0,3},{1,2},{2,1},{3,0},{4,7},{5,6},{6,5},{7,4},{8,11},{9,10},{10,... | collective-permute-start | bytes 1966088 | tf_op jit(solution)/shard_map/ppermute | solution.py:17
  73.1 41.5 %collective-permute-start.3 = (bf16[160,2048]{1,0:T(8,128)(2,1)}, bf16[160,2048]{1,0:T(8,128)(2,1)}, u32[]{:S(2)}, u32[]{:S(2)}) collective-permute-start(bf16[160,2048]{1,0:T(8,128)(2,1)} %get-tuple-element.66), channel_id=1, source_target_pairs={{0,2},{1,3},{2,0},{3,1},{4,6},{5,7},{6,4},{7,5},{8,10},{9,11},{10,... | collective-permute-start | bytes 1966088 | tf_op jit(solution)/shard_map/ppermute | solution.py:17
  73.8 40.8 %copy-start.22 = (bf16[160,2048]{1,0:T(8,128)(2,1)S(1)}, bf16[160,2048]{1,0:T(8,128)(2,1)}, u32[]{:S(2)}) copy-start(bf16[160,2048]{1,0:T(8,128)(2,1)} %get-tuple-element.67) | copy-start | bytes 1966084
  88.6 47.9 %copy-start.21 = (bf16[2,176,2048]{2,1,0:T(8,128)(2,1)}, bf16[2,176,2048]{2,1,0:T(8,128)(2,1)S(1)}, u32[]{:S(2)}) copy-start(bf16[2,176,2048]{2,1,0:T(8,128)(2,1)S(1)} %fusion.6) | copy-start | bytes 4325380
  122.5 14.1 %copy-start.5 = (f32[3,320,512]{2,1,0:T(8,128)}, f32[3,320,512]{2,1,0:T(8,128)S(1)}, u32[]{:S(2)}) copy-start(f32[3,320,512]{2,1,0:T(8,128)S(1)} %get-tuple-element.30) | copy-start | bytes 5898244
  122.5 14.1 %collective-permute-start.4 = (bf16[3,320,512]{2,1,0:T(8,128)(2,1)S(1)}, bf16[3,320,512]{2,1,0:T(8,128)(2,1)S(1)}, u32[]{:S(2)}, u32[]{:S(2)}) collective-permute-start(bf16[3,320,512]{2,1,0:T(8,128)(2,1)S(1)} %get-tuple-element.31), channel_id=1, source_target_pairs={{0,1},{1,0},{2,3},{3,2},{4,5},{5,4},{6,7},{7,6},{8,9},{9,8},{10,11... | collective-permute-start | bytes 2949128 | tf_op jit(solution)/shard_map/ppermute | solution.py:17
  129.4 9.1 %copy-start.3 = (f32[3,320,512]{2,1,0:T(8,128)}, f32[3,320,512]{2,1,0:T(8,128)S(1)}, u32[]{:S(2)}) copy-start(f32[3,320,512]{2,1,0:T(8,128)S(1)} %get-tuple-element.34) | copy-start | bytes 5898244
  129.5 9.1 %collective-permute-start.9 = (bf16[3,320,512]{2,1,0:T(8,128)(2,1)S(1)}, bf16[3,320,512]{2,1,0:T(8,128)(2,1)S(1)}, u32[]{:S(2)}, u32[]{:S(2)}) collective-permute-start(bf16[3,320,512]{2,1,0:T(8,128)(2,1)S(1)} %get-tuple-element.35), channel_id=1, source_target_pairs={{0,1},{1,0},{2,3},{3,2},{4,5},{5,4},{6,7},{7,6},{8,9},{9,8},{10,11... | collective-permute-start | bytes 2949128 | tf_op jit(solution)/shard_map/ppermute | solution.py:17
  136.4 3.7 %copy-start.1 = (f32[3,320,512]{2,1,0:T(8,128)}, f32[3,320,512]{2,1,0:T(8,128)S(1)}, u32[]{:S(2)}) copy-start(f32[3,320,512]{2,1,0:T(8,128)S(1)} %get-tuple-element.32) | copy-start | bytes 5898244
  136.4 3.7 %collective-permute-start.7 = (bf16[3,320,512]{2,1,0:T(8,128)(2,1)S(1)}, bf16[3,320,512]{2,1,0:T(8,128)(2,1)S(1)}, u32[]{:S(2)}, u32[]{:S(2)}) collective-permute-start(bf16[3,320,512]{2,1,0:T(8,128)(2,1)S(1)} %get-tuple-element.33), channel_id=1, source_target_pairs={{0,1},{1,0},{2,3},{3,2},{4,5},{5,4},{6,7},{7,6},{8,9},{9,8},{10,11... | collective-permute-start | bytes 2949128 | tf_op jit(solution)/shard_map/ppermute | solution.py:17
  136.6 4.7 %copy-start.11 = (bf16[3,320,512]{2,1,0:T(8,128)(2,1)}, bf16[3,320,512]{2,1,0:T(8,128)(2,1)S(1)}, u32[]{:S(2)}) copy-start(bf16[3,320,512]{2,1,0:T(8,128)(2,1)S(1)} %collective-permute-done.4) | copy-start | bytes 2949124
  136.8 14.1 %collective-permute-start.5 = (bf16[3,1,160,512]{3,2,1,0:T(8,128)(2,1)S(1)}, bf16[3,1,160,512]{3,2,1,0:T(8,128)(2,1)S(1)}, u32[]{:S(2)}, u32[]{:S(2)}) collective-permute-start(bf16[3,1,160,512]{3,2,1,0:T(8,128)(2,1)S(1)} %fusion.14), channel_id=1, source_target_pairs={{0,2},{1,3},{2,0},{3,1},{4,6},{5,7},{6,4},{7,5},{8,10},{9,11},{10,... | collective-permute-start | bytes 1474568 | tf_op jit(solution)/shard_map/ppermute | solution.py:17
  138.6 12.3 %copy-start.9 = (bf16[3,320,512]{2,1,0:T(8,128)(2,1)}, bf16[3,320,512]{2,1,0:T(8,128)(2,1)S(1)}, u32[]{:S(2)}) copy-start(bf16[3,320,512]{2,1,0:T(8,128)(2,1)S(1)} %collective-permute-done.9) | copy-start | bytes 2949124
  139.7 28.9 %collective-permute-start.10 = (bf16[3,1,160,512]{3,2,1,0:T(8,128)(2,1)}, bf16[3,1,160,512]{3,2,1,0:T(8,128)(2,1)}, u32[]{:S(2)}, u32[]{:S(2)}) collective-permute-start(bf16[3,1,160,512]{3,2,1,0:T(8,128)(2,1)} %fusion.12), channel_id=1, source_target_pairs={{0,2},{1,3},{2,0},{3,1},{4,6},{5,7},{6,4},{7,5},{8,10},{9,11},{10,... | collective-permute-start | bytes 1474568 | tf_op jit(solution)/shard_map/ppermute | solution.py:17
  140.1 2.6 copy-start.7
  141.2 31.3 %collective-permute-start.8 = (bf16[3,1,160,512]{3,2,1,0:T(8,128)(2,1)}, bf16[3,1,160,512]{3,2,1,0:T(8,128)(2,1)}, u32[]{:S(2)}, u32[]{:S(2)}) collective-permute-start(bf16[3,1,160,512]{3,2,1,0:T(8,128)(2,1)} %fusion.13), channel_id=1, source_target_pairs={{0,2},{1,3},{2,0},{3,1},{4,6},{5,7},{6,4},{7,5},{8,10},{9,11},{10,... | collective-permute-start | bytes 1474568 | tf_op jit(solution)/shard_map/ppermute | solution.py:17
  150.9 0.8 copy-start.14
  157.9 0.9 copy-start.16
  158.8 2.5 copy-start.20
  162.1 3.7 %copy-start = (f32[3,7,2048]{2,1,0:T(8,128)S(1)}, f32[3,7,2048]{2,1,0:T(8,128)}, u32[]{:S(2)}) copy-start(f32[3,7,2048]{2,1,0:T(8,128)} %refs_5_.15) | copy-start | bytes 516100
  162.1 3.7 %copy-start.6 = (f32[3,320,512]{2,1,0:T(8,128)S(1)}, f32[3,320,512]{2,1,0:T(8,128)}, u32[]{:S(2)}) copy-start(f32[3,320,512]{2,1,0:T(8,128)} %copy-done.5) | copy-start | bytes 5898244
  162.1 3.7 %copy-start.12 = (bf16[3,320,512]{2,1,0:T(8,128)(2,1)S(1)}, bf16[3,320,512]{2,1,0:T(8,128)(2,1)}, u32[]{:S(2)}) copy-start(bf16[3,320,512]{2,1,0:T(8,128)(2,1)} %copy-done.11) | copy-start | bytes 2949124
  162.1 3.7 %copy-start.13 = (f32[2048]{0:T(1024)S(1)}, f32[2048]{0:T(1024)}, u32[]{:S(2)}) copy-start(f32[2048]{0:T(1024)} %param.15) | copy-start | bytes 24580
  162.1 3.7 %copy-start.15 = (bf16[3,1,160,512]{3,2,1,0:T(8,128)(2,1)S(1)}, bf16[3,1,160,512]{3,2,1,0:T(8,128)(2,1)}, u32[]{:S(2)}) copy-start(bf16[3,1,160,512]{3,2,1,0:T(8,128)(2,1)} %copy-done.14) | copy-start | bytes 1474564
  162.3 13.8 %collective-permute-start.13 = (bf16[160,2048]{1,0:T(8,128)(2,1)S(1)}, bf16[160,2048]{1,0:T(8,128)(2,1)S(1)}, u32[]{:S(2)}, u32[]{:S(2)}) collective-permute-start(bf16[160,2048]{1,0:T(8,128)(2,1)S(1)} %get-tuple-element.61), channel_id=1, source_target_pairs={{0,1},{1,0},{2,3},{3,2},{4,5},{5,4},{6,7},{7,6},{8,9},{9,8},{10,11... | collective-permute-start | bytes 1966088 | tf_op jit(solution)/shard_map/ppermute | solution.py:17
  162.4 22.8 %collective-permute-start.14 = (bf16[160,2048]{1,0:T(8,128)(2,1)S(1)}, bf16[160,2048]{1,0:T(8,128)(2,1)S(1)}, u32[]{:S(2)}, u32[]{:S(2)}) collective-permute-start(bf16[160,2048]{1,0:T(8,128)(2,1)S(1)} %get-tuple-element.64), channel_id=1, source_target_pairs={{0,3},{1,2},{2,1},{3,0},{4,7},{5,6},{6,5},{7,4},{8,11},{9,10},{10,... | collective-permute-start | bytes 1966088 | tf_op jit(solution)/shard_map/ppermute | solution.py:17
  164.3 4.3 %copy-start.17 = (bf16[3,320,512]{2,1,0:T(8,128)(2,1)S(1)}, bf16[3,320,512]{2,1,0:T(8,128)(2,1)}, u32[]{:S(2)}) copy-start(bf16[3,320,512]{2,1,0:T(8,128)(2,1)} %copy-done.16) | copy-start | bytes 2949124
  164.3 4.4 %copy-start.4 = (f32[3,320,512]{2,1,0:T(8,128)S(1)}, f32[3,320,512]{2,1,0:T(8,128)}, u32[]{:S(2)}) copy-start(f32[3,320,512]{2,1,0:T(8,128)} %copy-done.3) | copy-start | bytes 5898244
  164.3 4.4 %copy-start.10 = (bf16[3,320,512]{2,1,0:T(8,128)(2,1)S(1)}, bf16[3,320,512]{2,1,0:T(8,128)(2,1)}, u32[]{:S(2)}) copy-start(bf16[3,320,512]{2,1,0:T(8,128)(2,1)} %copy-done.9) | copy-start | bytes 2949124
  164.3 35.3 %collective-permute-start.15 = (bf16[160,2048]{1,0:T(8,128)(2,1)S(1)}, bf16[160,2048]{1,0:T(8,128)(2,1)S(1)}, u32[]{:S(2)}, u32[]{:S(2)}) collective-permute-start(bf16[160,2048]{1,0:T(8,128)(2,1)S(1)} %get-tuple-element.62), channel_id=1, source_target_pairs={{0,2},{1,3},{2,0},{3,1},{4,6},{5,7},{6,4},{7,5},{8,10},{9,11},{10,... | collective-permute-start | bytes 1966088 | tf_op jit(solution)/shard_map/ppermute | solution.py:17
  168.5 4.1 %copy-start.2 = (f32[3,320,512]{2,1,0:T(8,128)S(1)}, f32[3,320,512]{2,1,0:T(8,128)}, u32[]{:S(2)}) copy-start(f32[3,320,512]{2,1,0:T(8,128)} %copy-done.1) | copy-start | bytes 5898244
  168.5 4.1 %copy-start.8 = (bf16[3,320,512]{2,1,0:T(8,128)(2,1)S(1)}, bf16[3,320,512]{2,1,0:T(8,128)(2,1)}, u32[]{:S(2)}) copy-start(bf16[3,320,512]{2,1,0:T(8,128)(2,1)} %copy-done.7) | copy-start | bytes 2949124
  168.5 37.6 %collective-permute-start.11 = (bf16[3,320,512]{2,1,0:T(8,128)(2,1)S(1)}, bf16[3,320,512]{2,1,0:T(8,128)(2,1)S(1)}, u32[]{:S(2)}, u32[]{:S(2)}) collective-permute-start(bf16[3,320,512]{2,1,0:T(8,128)(2,1)S(1)} %copy-done.17), channel_id=1, source_target_pairs={{0,1},{1,0},{2,3},{3,2},{4,5},{5,4},{6,7},{7,6},{8,9},{9,8},{10,11... | collective-permute-start | bytes 2949128 | tf_op jit(solution)/shard_map/ppermute | solution.py:17
  206.1 2.6 collective-permute-start.16
  206.3 14.1 %collective-permute-start.12 = (bf16[3,1,160,512]{3,2,1,0:T(8,128)(2,1)S(1)}, bf16[3,1,160,512]{3,2,1,0:T(8,128)(2,1)S(1)}, u32[]{:S(2)}, u32[]{:S(2)}) collective-permute-start(bf16[3,1,160,512]{3,2,1,0:T(8,128)(2,1)S(1)} %fusion.11), channel_id=1, source_target_pairs={{0,2},{1,3},{2,0},{3,1},{4,6},{5,7},{6,4},{7,5},{8,10},{9,11},{10,... | collective-permute-start | bytes 1474568 | tf_op jit(solution)/shard_map/ppermute | solution.py:17
  208.9 21.7 %collective-permute-start.17 = (bf16[3,1,160,512]{3,2,1,0:T(8,128)(2,1)S(1)}, bf16[3,1,160,512]{3,2,1,0:T(8,128)(2,1)S(1)}, u32[]{:S(2)}, u32[]{:S(2)}) collective-permute-start(bf16[3,1,160,512]{3,2,1,0:T(8,128)(2,1)S(1)} %fusion.10), channel_id=1, source_target_pairs={{0,2},{1,3},{2,0},{3,1},{4,6},{5,7},{6,4},{7,5},{8,10},{9,11},{10,... | collective-permute-start | bytes 1474568 | tf_op jit(solution)/shard_map/ppermute | solution.py:17
  216.9 20.0 %collective-permute-start.18 = (bf16[3,320,512]{2,1,0:T(8,128)(2,1)S(1)}, bf16[3,320,512]{2,1,0:T(8,128)(2,1)S(1)}, u32[]{:S(2)}, u32[]{:S(2)}) collective-permute-start(bf16[3,320,512]{2,1,0:T(8,128)(2,1)S(1)} %get-tuple-element.46), channel_id=1, source_target_pairs={{0,1},{1,0},{2,3},{3,2},{4,5},{5,4},{6,7},{7,6},{8,9},{9,8},{10,11... | collective-permute-start | bytes 2949128 | tf_op jit(solution)/shard_map/ppermute | solution.py:17
  226.6 12.2 %collective-permute-start.20 = (bf16[3,320,512]{2,1,0:T(8,128)(2,1)S(1)}, bf16[3,320,512]{2,1,0:T(8,128)(2,1)S(1)}, u32[]{:S(2)}, u32[]{:S(2)}) collective-permute-start(bf16[3,320,512]{2,1,0:T(8,128)(2,1)S(1)} %get-tuple-element.49), channel_id=1, source_target_pairs={{0,1},{1,0},{2,3},{3,2},{4,5},{5,4},{6,7},{7,6},{8,9},{9,8},{10,11... | collective-permute-start | bytes 2949128 | tf_op jit(solution)/shard_map/ppermute | solution.py:17
  236.8 2.6 collective-permute-start.22
  237.0 14.1 %collective-permute-start.19 = (bf16[3,1,160,512]{3,2,1,0:T(8,128)(2,1)S(1)}, bf16[3,1,160,512]{3,2,1,0:T(8,128)(2,1)S(1)}, u32[]{:S(2)}, u32[]{:S(2)}) collective-permute-start(bf16[3,1,160,512]{3,2,1,0:T(8,128)(2,1)S(1)} %fusion.9), channel_id=1, source_target_pairs={{0,2},{1,3},{2,0},{3,1},{4,6},{5,7},{6,4},{7,5},{8,10},{9,11},{10,... | collective-permute-start | bytes 1474568 | tf_op jit(solution)/shard_map/ppermute | solution.py:17
  239.0 22.6 %collective-permute-start.21 = (bf16[3,1,160,512]{3,2,1,0:T(8,128)(2,1)S(1)}, bf16[3,1,160,512]{3,2,1,0:T(8,128)(2,1)S(1)}, u32[]{:S(2)}, u32[]{:S(2)}) collective-permute-start(bf16[3,1,160,512]{3,2,1,0:T(8,128)(2,1)S(1)} %fusion.8), channel_id=1, source_target_pairs={{0,2},{1,3},{2,0},{3,1},{4,6},{5,7},{6,4},{7,5},{8,10},{9,11},{10,... | collective-permute-start | bytes 1474568 | tf_op jit(solution)/shard_map/ppermute | solution.py:17
  239.6 32.2 %collective-permute-start.23 = (bf16[3,1,160,512]{3,2,1,0:T(8,128)(2,1)S(1)}, bf16[3,1,160,512]{3,2,1,0:T(8,128)(2,1)S(1)}, u32[]{:S(2)}, u32[]{:S(2)}) collective-permute-start(bf16[3,1,160,512]{3,2,1,0:T(8,128)(2,1)S(1)} %fusion.7), channel_id=1, source_target_pairs={{0,2},{1,3},{2,0},{3,1},{4,6},{5,7},{6,4},{7,5},{8,10},{9,11},{10,... | collective-permute-start | bytes 1474568 | tf_op jit(solution)/shard_map/ppermute | solution.py:17
Sparse Core Ops, SparseCore 0:
  9.2 57.4 all-gather.2
  68.3 53.5 all-gather.4
